TPU v7x, 256 devices: a whole 4x4x8 slice. The times are simulated.
256 devices in a mesh: dp: 4 (over z_lo), row: 4 (over x), col: 16 (over z_hi, y, core).
Axes of the slice: x: 4, y: 4, z: 8 (z_hi: 2, z_lo: 4; z = z_hi * 4 + z_lo), core: 2. Of those that a mesh axis runs over, the one named last changes fastest.
Arguments:
- activations: bfloat16 [4096, 8192], P('dp', 'row'), may hold values from -6 to 6
- grad_out: bfloat16 [4096, 26624], P('dp', 'col'), may hold values from -0.09375 to 0.09375
- sketch: float32 [26624, 128], P('col'), may hold values from -6 to 6
Outputs:
- basis: float32 [8192, 128], P('row')
- coef: float32 [128, 26624], P(None, 'col')
All inputs are finite; a program needn't handle non-finite values.
Results may differ from a plain program's by a relative error of at most 0.0003.
Values sent between devices are 32-bit elements; how exact they have to be, the bound alone decides.
A program may use at most 128 MiB of HBM per device.

v0:
```python
import math

import jax
import jax.numpy as jnp
from jax import lax
from jax.sharding import PartitionSpec as P

D = 8192
ITERS = 2


def cholesky_basis(mat, gram):
    lower = jnp.linalg.cholesky(gram)
    return jax.scipy.linalg.solve_triangular(lower, mat.T, lower=True).T


def body(activations, grad_out, sketch):
    hp = lax.Precision.HIGHEST
    piece = lax.psum_scatter(
        jnp.einsum("tk,tf->kf", activations, grad_out, preferred_element_type=jnp.float32),
        "dp",
        scatter_dimension=0,
        tiled=True,
    )

    def range_basis(mat):
        rows_part = lax.psum(jnp.dot(piece, mat, precision=hp), "col")
        gram = lax.psum(jnp.dot(rows_part.T, rows_part, precision=hp), ("dp", "row"))
        return cholesky_basis(rows_part, gram)

    basis_part = range_basis(sketch)
    for step in range(ITERS):
        basis_part = range_basis(
            lax.psum(jnp.dot(piece.T, basis_part, precision=hp), ("dp", "row"))
        )
    coef = lax.psum(jnp.dot(basis_part.T, piece, precision=hp), ("dp", "row"))
    basis = lax.all_gather(basis_part, "dp", axis=0, tiled=True)
    return (basis * math.sqrt(D), coef)


def solution(mesh):
    in_specs = (P("dp", "row"), P("dp", "col"), P("col", None))
    out_specs = (P("row", None), P(None, "col"))
    return jax.shard_map(body, mesh=mesh, in_specs=in_specs, out_specs=out_specs, check_vma=False)
```

profile of v0, /device:TPU:1, one launch (start us, length us, event | category | flops | bytes accessed | tf_op | source)
XLA Modules:
  0.0 1870.1 jit_solution(3224131129523955086)
XLA Ops:
  7.2 1.9 copy-done
  9.1 12.5 fusion.19
  21.7 237.9 %reduce-scatter.2.cloned.1.call-done = f32[512,1664]{1,0:T(8,128)} async-done(((f32[2048,1664]{1,0:T(8,128)}), f32[512,1664]{1,0:T(8,128)}) %reduce-scatter.2.cloned.1.call-update) | async-done | bytes 3407888 | tf_op jit(solution)/shard_map/reduce_scatter | solution.py:19
  259.6 5.8 fusion.20
  265.5 177.7 %all-reduce.10.cloned.1.call-done = f32[512,128]{1,0:T(8,128)} async-done(((f32[512,128]{1,0:T(8,128)}), f32[512,128]{1,0:T(8,128)}) %all-reduce.10.cloned.1.call-update) | async-done | bytes 262160 | tf_op jit(solution)/shard_map/psum | solution.py:27
  443.1 2.2 fusion.21
  445.6 141.0 %all-reduce.12.cloned.1.call-done = f32[128,128]{0,1:T(8,128)} async-done(((f32[128,128]{0,1:T(8,128)}), f32[128,128]{0,1:T(8,128)}) %all-reduce.12.cloned.1.call-update) | async-done | bytes 65552 | tf_op jit(solution)/shard_map/psum | solution.py:28
  588.4 11.7 cholesky.59
  601.5 9.8 custom-call.7
  612.7 8.3 fusion.22
  621.1 158.6 %all-reduce.14.cloned.1.call-done = f32[1664,128]{1,0:T(8,128)} async-done(((f32[1664,128]{1,0:T(8,128)}), f32[1664,128]{1,0:T(8,128)}) %all-reduce.14.cloned.1.call-update) | async-done | bytes 851984 | tf_op jit(solution)/shard_map/psum | solution.py:34
  779.7 5.8 fusion.23
  785.6 184.3 %all-reduce.16.cloned.1.call-done = f32[512,128]{1,0:T(8,128)} async-done(((f32[512,128]{1,0:T(8,128)}), f32[512,128]{1,0:T(8,128)}) %all-reduce.16.cloned.1.call-update) | async-done | bytes 262160 | tf_op jit(solution)/shard_map/psum | solution.py:27
  969.9 2.2 fusion.24
  972.6 140.4 %all-reduce.18.cloned.1.call-done = f32[128,128]{0,1:T(8,128)} async-done(((f32[128,128]{0,1:T(8,128)}), f32[128,128]{0,1:T(8,128)}) %all-reduce.18.cloned.1.call-update) | async-done | bytes 65552 | tf_op jit(solution)/shard_map/psum | solution.py:28
  1114.9 11.7 cholesky.70
  1127.9 9.8 custom-call.8
  1139.1 8.3 fusion.25
  1147.7 158.7 %all-reduce.20.cloned.1.call-done = f32[1664,128]{1,0:T(8,128)} async-done(((f32[1664,128]{1,0:T(8,128)}), f32[1664,128]{1,0:T(8,128)}) %all-reduce.20.cloned.1.call-update) | async-done | bytes 851984 | tf_op jit(solution)/shard_map/psum | solution.py:34
  1306.4 5.8 fusion.26
  1312.2 184.2 %all-reduce.22.cloned.1.call-done = f32[512,128]{1,0:T(8,128)} async-done(((f32[512,128]{1,0:T(8,128)}), f32[512,128]{1,0:T(8,128)}) %all-reduce.22.cloned.1.call-update) | async-done | bytes 262160 | tf_op jit(solution)/shard_map/psum | solution.py:27
  1496.5 2.2 fusion.27
  1498.8 141.2 %all-reduce.24.cloned.1.call-done = f32[128,128]{0,1:T(8,128)} async-done(((f32[128,128]{0,1:T(8,128)}), f32[128,128]{0,1:T(8,128)}) %all-reduce.24.cloned.1.call-update) | async-done | bytes 65552 | tf_op jit(solution)/shard_map/psum | solution.py:28
  1641.8 11.7 cholesky.81
  1654.8 9.8 custom-call.9
  1664.6 2.1 fusion
  1667.0 5.0 fusion.28
  1672.0 34.3 %all-gather.2.cloned.1.call-done = f32[2048,128]{0,1:T(8,128)} async-done(((f32[512,128]{0,1:T(8,128)}), f32[2048,128]{0,1:T(8,128)}) %all-gather.2.cloned.1.call-update) | async-done | bytes 1048592 | tf_op jit(solution)/shard_map/all_gather | solution.py:37
  1706.3 2.4 broadcast_multiply_fusion
  1708.6 2.5 copy.11
  1711.2 150.1 %all-reduce.26.cloned.1.call-done = f32[128,1664]{1,0:T(8,128)} async-done(((f32[128,1664]{1,0:T(8,128)}), f32[128,1664]{1,0:T(8,128)}) %all-reduce.26.cloned.1.call-update) | async-done | bytes 851984 | tf_op jit(solution)/shard_map/psum | solution.py:36
  1861.2 2.1 copy.24
  (40 shorter events, 13.7 us)
Async XLA Ops:
  7.2 2.0 copy-start
  7.2 252.4 %reduce-scatter.2.cloned.1.call-start = ((), (), s32[]{:S(2)}) async-start(), calls=%async_computation.1 | async-start | bytes 17039360 | tf_op jit(solution)/shard_map/reduce_scatter | solution.py:19
  21.7 421.4 %all-reduce.10.cloned.1.call-start = ((), (), s32[]{:S(2)}) async-start(), calls=%async_computation.2 | async-start | bytes 524288 | tf_op jit(solution)/shard_map/psum | solution.py:27
  265.4 321.2 %all-reduce.12.cloned.1.call-start = ((), (), s32[]{:S(2)}) async-start(), calls=%async_computation.3 | async-start | bytes 131072 | tf_op jit(solution)/shard_map/psum | solution.py:28
  445.4 334.3 %all-reduce.14.cloned.1.call-start = ((), (), s32[]{:S(2)}) async-start(), calls=%async_computation.4 | async-start | bytes 1703936 | tf_op jit(solution)/shard_map/psum | solution.py:34
  621.0 348.9 %all-reduce.16.cloned.1.call-start = ((), (), s32[]{:S(2)}) async-start(), calls=%async_computation.5 | async-start | bytes 524288 | tf_op jit(solution)/shard_map/psum | solution.py:27
  785.5 327.6 %all-reduce.18.cloned.1.call-start = ((), (), s32[]{:S(2)}) async-start(), calls=%async_computation.6 | async-start | bytes 131072 | tf_op jit(solution)/shard_map/psum | solution.py:28
  972.2 334.2 %all-reduce.20.cloned.1.call-start = ((), (), s32[]{:S(2)}) async-start(), calls=%async_computation.7 | async-start | bytes 1703936 | tf_op jit(solution)/shard_map/psum | solution.py:34
  1147.5 349.0 %all-reduce.22.cloned.1.call-start = ((), (), s32[]{:S(2)}) async-start(), calls=%async_computation.8 | async-start | bytes 524288 | tf_op jit(solution)/shard_map/psum | solution.py:27
  1312.2 327.8 %all-reduce.24.cloned.1.call-start = ((), (), s32[]{:S(2)}) async-start(), calls=%async_computation.9 | async-start | bytes 131072 | tf_op jit(solution)/shard_map/psum | solution.py:28
  1498.7 207.5 %all-gather.2.cloned.1.call-start = ((), (), s32[]{:S(2)}) async-start(), calls=%async_computation.10 | async-start | bytes 1310720 | tf_op jit(solution)/shard_map/all_gather | solution.py:37
  1666.7 194.5 %all-reduce.26.cloned.1.call-start = ((), (), s32[]{:S(2)}) async-start(), calls=%async_computation.11 | async-start | bytes 1703936 | tf_op jit(solution)/shard_map/psum | solution.py:36
Sparse Core Ops, SparseCore 0:
  21.8 237.7 reduce-scatter.1
  265.5 177.5 all-reduce.9
  446.5 140.0 all-reduce.11
  621.2 158.5 all-reduce.13
  785.6 184.2 all-reduce.15
  972.9 140.0 all-reduce.17
  1147.6 158.7 all-reduce.19
  1312.3 184.0 all-reduce.21
  1499.8 140.0 all-reduce.23
  1666.9 39.3 all-gather.1
  1709.5 151.7 all-reduce.25
where the time goes:
time: 1890 us; the launch traced here: 1870 us
  waiting for transfers between devices  1710 us (90%)
  other arithmetic  73.5 us (4%)
  matrix products  63 us (3%)
    psum x3, waiting for transfers between devices, range_basis(): rows_part = lax.psum(jnp.dot(piece, mat, precision=hp), 'col')  546 us
    psum x3, waiting for transfers between devices, range_basis(): lax.psum(jnp.dot(rows_part.T, rows_part, precision=hp), ('dp', 'row'))  423 us
    psum x2, waiting for transfers between devices, body(): lax.psum(jnp.dot(piece.T, basis_part, precision=hp), ('dp', 'row'))  317 us
    reduce_scatter x1, waiting for transfers between devices, body(): lax.psum_scatter(jnp.einsum('tk,tf->kf', activations, grad_out, preferred...  238 us
    psum x1, waiting for transfers between devices, body(): coef = lax.psum(jnp.dot(basis_part.T, piece, precision=hp), ('dp', 'row'))  150 us
  transfers between devices with their start and end apart: 11, of which 11 were waited for; matrix products, arithmetic and copies ran while one was open for 1% of the time, Pallas kernels for 0%

commit v1 on v0

v1 whole, which is shorter than its diff:
```python
import math

import jax
import jax.numpy as jnp
from jax import lax
from jax.sharding import PartitionSpec as P

D = 8192
ITERS = 2


def halves(mat):
    high = lax.reduce_precision(mat, 8, 7)
    low = lax.reduce_precision(mat - high, 8, 7)
    return jnp.concatenate([high.astype(jnp.bfloat16), low.astype(jnp.bfloat16)], axis=1)


def product(lhs, mat, dim):
    wide = lax.dot_general(
        lhs, halves(mat), (((dim,), (0,)), ((), ())), preferred_element_type=jnp.float32
    )
    rank = mat.shape[1]
    return wide[:, :rank] + wide[:, rank:]


def body(activations, grad_out, sketch):
    hp = lax.Precision.HIGHEST

    def apply_grad(mat):
        tokens = lax.psum(product(grad_out, mat, 1), "col")
        return lax.psum(product(activations, tokens, 0), "dp")

    def apply_trans(mat):
        tokens = lax.psum(product(activations, mat, 1), "row")
        return lax.psum(product(grad_out, tokens, 0), "dp")

    def orthonormal(mat):
        gram = lax.psum(jnp.dot(mat.T, mat, precision=hp), "row")
        lower = jnp.linalg.cholesky(gram)
        inverse = jax.scipy.linalg.solve_triangular(
            lower, jnp.eye(lower.shape[0], dtype=jnp.float32), lower=True
        )
        return jnp.dot(mat, inverse.T, precision=hp)

    basis = orthonormal(apply_grad(sketch))
    for step in range(ITERS):
        basis = orthonormal(apply_grad(apply_trans(basis)))
    coef = apply_trans(basis).T
    return (basis * math.sqrt(D), coef)


def solution(mesh):
    in_specs = (P("dp", "row"), P("dp", "col"), P("col", None))
    out_specs = (P("row", None), P(None, "col"))
    return jax.shard_map(body, mesh=mesh, in_specs=in_specs, out_specs=out_specs, check_vma=False)
```

time: 1890 us -> 1350 us (0.71)
  waiting for transfers between devices: 1710 us -> 1190 us
  other arithmetic: 73.5 us -> 93.1 us
    psum x9 -> x15, waiting for transfers between devices: 1440 us -> 1190 us  [the longest x3 535 us: apply_grad(): tokens = lax.psum(product(grad_out, mat, 1), 'col')]
    reduce_scatter x1 -> x0, waiting for transfers between devices: 238 us -> none  [body(): lax.psum_scatter(jnp.einsum('tk,tf->kf', activations, grad_out, preferred...]
    all_gather x1 -> x0, waiting for transfers between devices: 34.3 us -> none  [body(): basis = lax.all_gather(basis_part, 'dp', axis=0, tiled=True)]
    dot_general x10 -> x18, matrix products: 58.2 us -> 45.2 us  [the longest x12 27.7 us: product(): lax.dot_general(lhs, halves(mat), (((dim,), (0,)), ((), ())), preferred_e...]
  transfers between devices with their start and end apart: 11 -> 15, of which waited for: 11 -> 15; matrix products, arithmetic and copies ran while one was open for 1% -> 0% of each run, Pallas kernels for 0% -> 0%
where the time goes in v1:
time: 1350 us
  waiting for transfers between devices  1190 us (88%)
  other arithmetic  93.1 us (7%)
  matrix products  46.1 us (3%)
  between operations  14.4 us (1%)
    psum x3, waiting for transfers between devices, apply_grad(): tokens = lax.psum(product(grad_out, mat, 1), 'col')  535 us
    psum x3, waiting for transfers between devices, apply_grad(): return lax.psum(product(activations, tokens, 0), 'dp')  194 us
    psum x3, waiting for transfers between devices, apply_trans(): return lax.psum(product(grad_out, tokens, 0), 'dp')  181 us
    psum x3, waiting for transfers between devices, apply_trans(): tokens = lax.psum(product(activations, mat, 1), 'row')  146 us
    psum x3, waiting for transfers between devices, orthonormal(): gram = lax.psum(jnp.dot(mat.T, mat, precision=hp), 'row')  129 us
    another operation x9, other arithmetic, orthonormal(): lower = jnp.linalg.cholesky(gram)  37.2 us
    another operation x6, other arithmetic, orthonormal(): jax.scipy.linalg.solve_triangular(lower, jnp.eye(lower.shape[0], dtype=jn...  31.4 us
    dot_general x12, matrix products, product(): lax.dot_general(lhs, halves(mat), (((dim,), (0,)), ((), ())), preferred_e...  27.7 us
  transfers between devices with their start and end apart: 15, of which 15 were waited for; matrix products, arithmetic and copies ran while one was open for 0% of the time, Pallas kernels for 0%

profile of v1, /device:TPU:1, one launch (start us, length us, event | category | flops | bytes accessed | tf_op | source)
XLA Modules:
  0.0 1348.9 jit_solution(15702161839477209291)
XLA Ops:
  11.5 181.5 %all-reduce.16.cloned.1.call-done = f32[1024,128]{0,1:T(8,128)} async-done(((f32[1024,128]{0,1:T(8,128)}), f32[1024,128]{0,1:T(8,128)}) %all-reduce.16.cloned.1.call-update) | async-done | bytes 524304 | tf_op jit(solution)/shard_map/psum | solution.py:30
  194.1 3.5 convolution_bitcast_fusion.5
  198.8 64.7 %all-reduce.18.cloned.1.call-done = f32[2048,128]{0,1:T(8,128)} async-done(((f32[2048,128]{0,1:T(8,128)}), f32[2048,128]{0,1:T(8,128)}) %all-reduce.18.cloned.1.call-update) | async-done | bytes 1048592 | tf_op jit(solution)/shard_map/psum | solution.py:31
  263.4 3.2 fusion.88
  267.2 42.7 %all-reduce.20.cloned.1.call-done = f32[128,128]{0,1:T(8,128)} async-done(((f32[128,128]{0,1:T(8,128)}), f32[128,128]{0,1:T(8,128)}) %all-reduce.20.cloned.1.call-update) | async-done | bytes 65552 | tf_op jit(solution)/shard_map/psum | solution.py:38
  311.6 11.7 cholesky.59
  324.7 9.8 custom-call.7
  337.1 3.5 convolution_bitcast_fusion.10
  341.5 48.8 %all-reduce.22.cloned.1.call-done = f32[1024,128]{0,1:T(8,128)} async-done(((f32[1024,128]{0,1:T(8,128)}), f32[1024,128]{0,1:T(8,128)}) %all-reduce.22.cloned.1.call-update) | async-done | bytes 524304 | tf_op jit(solution)/shard_map/psum | solution.py:34
  393.6 61.1 %all-reduce.24.cloned.1.call-done = f32[1664,128]{0,1:T(8,128)} async-done(((f32[1664,128]{0,1:T(8,128)}), f32[1664,128]{0,1:T(8,128)}) %all-reduce.24.cloned.1.call-update) | async-done | bytes 851984 | tf_op jit(solution)/shard_map/psum | solution.py:35
  458.0 177.1 %all-reduce.26.cloned.1.call-done = f32[1024,128]{0,1:T(8,128)} async-done(((f32[1024,128]{0,1:T(8,128)}), f32[1024,128]{0,1:T(8,128)}) %all-reduce.26.cloned.1.call-update) | async-done | bytes 524304 | tf_op jit(solution)/shard_map/psum | solution.py:30
  636.2 3.5 convolution_bitcast_fusion.4
  641.0 64.5 %all-reduce.28.cloned.1.call-done = f32[2048,128]{0,1:T(8,128)} async-done(((f32[2048,128]{0,1:T(8,128)}), f32[2048,128]{0,1:T(8,128)}) %all-reduce.28.cloned.1.call-update) | async-done | bytes 1048592 | tf_op jit(solution)/shard_map/psum | solution.py:31
  705.6 3.2 fusion.89
  708.8 43.2 %all-reduce.30.cloned.1.call-done = f32[128,128]{0,1:T(8,128)} async-done(((f32[128,128]{0,1:T(8,128)}), f32[128,128]{0,1:T(8,128)}) %all-reduce.30.cloned.1.call-update) | async-done | bytes 65552 | tf_op jit(solution)/shard_map/psum | solution.py:38
  753.8 11.7 cholesky.70
  766.8 9.8 custom-call.8
  779.2 3.5 convolution_bitcast_fusion.8
  783.6 48.8 %all-reduce.32.cloned.1.call-done = f32[1024,128]{0,1:T(8,128)} async-done(((f32[1024,128]{0,1:T(8,128)}), f32[1024,128]{0,1:T(8,128)}) %all-reduce.32.cloned.1.call-update) | async-done | bytes 524304 | tf_op jit(solution)/shard_map/psum | solution.py:34
  835.7 61.1 %all-reduce.34.cloned.1.call-done = f32[1664,128]{0,1:T(8,128)} async-done(((f32[1664,128]{0,1:T(8,128)}), f32[1664,128]{0,1:T(8,128)}) %all-reduce.34.cloned.1.call-update) | async-done | bytes 851984 | tf_op jit(solution)/shard_map/psum | solution.py:35
  900.4 176.9 %all-reduce.36.cloned.1.call-done = f32[1024,128]{0,1:T(8,128)} async-done(((f32[1024,128]{0,1:T(8,128)}), f32[1024,128]{0,1:T(8,128)}) %all-reduce.36.cloned.1.call-update) | async-done | bytes 524304 | tf_op jit(solution)/shard_map/psum | solution.py:30
  1078.3 3.5 convolution_bitcast_fusion.3
  1083.0 64.7 %all-reduce.38.cloned.1.call-done = f32[2048,128]{0,1:T(8,128)} async-done(((f32[2048,128]{0,1:T(8,128)}), f32[2048,128]{0,1:T(8,128)}) %all-reduce.38.cloned.1.call-update) | async-done | bytes 1048592 | tf_op jit(solution)/shard_map/psum | solution.py:31
  1147.7 3.3 fusion.90
  1151.0 43.2 %all-reduce.40.cloned.1.call-done = f32[128,128]{0,1:T(8,128)} async-done(((f32[128,128]{0,1:T(8,128)}), f32[128,128]{0,1:T(8,128)}) %all-reduce.40.cloned.1.call-update) | async-done | bytes 65552 | tf_op jit(solution)/shard_map/psum | solution.py:38
  1196.0 11.7 cholesky.81
  1209.0 9.8 custom-call.9
  1219.1 3.4 reduce-precision_convert_fusion
  1222.5 3.5 convolution_bitcast_fusion.6
  1226.9 48.8 %all-reduce.42.cloned.1.call-done = f32[1024,128]{0,1:T(8,128)} async-done(((f32[1024,128]{0,1:T(8,128)}), f32[1024,128]{0,1:T(8,128)}) %all-reduce.42.cloned.1.call-update) | async-done | bytes 524304 | tf_op jit(solution)/shard_map/psum | solution.py:34
  1279.0 2.5 copy.11
  1281.5 58.6 %all-reduce.44.cloned.1.call-done = f32[128,1664]{1,0:T(8,128)} async-done(((f32[128,1664]{1,0:T(8,128)}), f32[128,1664]{1,0:T(8,128)}) %all-reduce.44.cloned.1.call-update) | async-done | bytes 851984 | tf_op jit(solution)/shard_map/psum | solution.py:35
  (80 shorter events, 48.2 us)
Async XLA Ops:
  7.2 2.2 copy-start
  7.2 185.8 %all-reduce.16.cloned.1.call-start = ((), (), s32[]{:S(2)}) async-start(), calls=%async_computation | async-start | bytes 1048576 | tf_op jit(solution)/shard_map/psum | solution.py:30
  11.5 252.0 %all-reduce.18.cloned.1.call-start = ((), (), s32[]{:S(2)}) async-start(), calls=%async_computation.1 | async-start | bytes 2097152 | tf_op jit(solution)/shard_map/psum | solution.py:31
  198.7 111.1 %all-reduce.20.cloned.1.call-start = ((), (), s32[]{:S(2)}) async-start(), calls=%async_computation.2 | async-start | bytes 131072 | tf_op jit(solution)/shard_map/psum | solution.py:38
  266.6 123.7 %all-reduce.22.cloned.1.call-start = ((), (), s32[]{:S(2)}) async-start(), calls=%async_computation.3 | async-start | bytes 1048576 | tf_op jit(solution)/shard_map/psum | solution.py:34
  341.5 113.2 %all-reduce.24.cloned.1.call-start = ((), (), s32[]{:S(2)}) async-start(), calls=%async_computation.4 | async-start | bytes 1703936 | tf_op jit(solution)/shard_map/psum | solution.py:35
  393.6 241.5 %all-reduce.26.cloned.1.call-start = ((), (), s32[]{:S(2)}) async-start(), calls=%async_computation.5 | async-start | bytes 1048576 | tf_op jit(solution)/shard_map/psum | solution.py:30
  458.0 247.6 %all-reduce.28.cloned.1.call-start = ((), (), s32[]{:S(2)}) async-start(), calls=%async_computation.6 | async-start | bytes 2097152 | tf_op jit(solution)/shard_map/psum | solution.py:31
  640.8 111.1 %all-reduce.30.cloned.1.call-start = ((), (), s32[]{:S(2)}) async-start(), calls=%async_computation.7 | async-start | bytes 131072 | tf_op jit(solution)/shard_map/psum | solution.py:38
  708.8 123.7 %all-reduce.32.cloned.1.call-start = ((), (), s32[]{:S(2)}) async-start(), calls=%async_computation.8 | async-start | bytes 1048576 | tf_op jit(solution)/shard_map/psum | solution.py:34
  783.6 113.2 %all-reduce.34.cloned.1.call-start = ((), (), s32[]{:S(2)}) async-start(), calls=%async_computation.9 | async-start | bytes 1703936 | tf_op jit(solution)/shard_map/psum | solution.py:35
  835.7 241.5 %all-reduce.36.cloned.1.call-start = ((), (), s32[]{:S(2)}) async-start(), calls=%async_computation.10 | async-start | bytes 1048576 | tf_op jit(solution)/shard_map/psum | solution.py:30
  900.1 247.6 %all-reduce.38.cloned.1.call-start = ((), (), s32[]{:S(2)}) async-start(), calls=%async_computation.11 | async-start | bytes 2097152 | tf_op jit(solution)/shard_map/psum | solution.py:31
  1082.9 111.3 %all-reduce.40.cloned.1.call-start = ((), (), s32[]{:S(2)}) async-start(), calls=%async_computation.12 | async-start | bytes 131072 | tf_op jit(solution)/shard_map/psum | solution.py:38
  1151.0 124.7 %all-reduce.42.cloned.1.call-start = ((), (), s32[]{:S(2)}) async-start(), calls=%async_computation.13 | async-start | bytes 1048576 | tf_op jit(solution)/shard_map/psum | solution.py:34
  1226.8 113.2 %all-reduce.44.cloned.1.call-start = ((), (), s32[]{:S(2)}) async-start(), calls=%async_computation.14 | async-start | bytes 1703936 | tf_op jit(solution)/shard_map/psum | solution.py:35
Sparse Core Ops, SparseCore 0:
  11.6 181.3 all-reduce.15
  198.8 64.5 all-reduce.17
  266.8 43.0 all-reduce.19
  341.6 48.6 all-reduce.21
  393.7 60.9 all-reduce.23
  458.1 176.9 all-reduce.25
  640.9 64.5 all-reduce.27
  708.9 43.0 all-reduce.29
  783.7 48.6 all-reduce.31
  835.8 60.9 all-reduce.33
  900.2 176.9 all-reduce.35
  1083.0 64.5 all-reduce.37
  1151.1 43.0 all-reduce.39
  1227.0 48.6 all-reduce.41
  1279.1 60.9 all-reduce.43

commit v2 on v0

v2 whole, which is shorter than its diff:
```python
import functools
import math

import jax
import jax.numpy as jnp
from jax import lax
from jax.experimental import pallas as pl
from jax.experimental.pallas import tpu as pltpu
from jax.sharding import PartitionSpec as P

MESH = pl.DeviceIdType.MESH
F32 = jnp.float32
BF16 = jnp.bfloat16
HIGHEST = lax.Precision.HIGHEST
D = 8192
RANK = 128
ROUNDS = 3
TOK = 1024
HID = 1664
NN = (((1,), (0,)), ((), ()))
NT = (((1,), (1,)), ((), ()))
TN = (((0,), (0,)), ((), ()))
YC, YR, YG, YX, MZ, XC, XR, XG, XX, PR, PG, GC, GR, GX, GZ = range(15)
PHASES = 15
LA, LB, LS, FX, FB, FC = range(6)


def terms(mat):
    high = mat.astype(BF16)
    low = (mat - high.astype(F32)).astype(BF16)
    return high, low


def twice(mat):
    return jnp.concatenate(terms(mat), axis=0)


def folded(wide):
    rows = wide.shape[0] // 2
    return wide[:rows] + wide[rows:]


def kernel(
    a_hbm, b_hbm, s_hbm, basis_ref, coef_ref,
    a, at, b, s, st, pt, ysend, ycore, yown, yrs, yt, ylhs, mzs, mt, xs, xcore, xown, xrs, xt, xlhs,
    ps, prs, gown, gcore, gsum, grs, gpart, grx, gfull, work, linv, cf, mg,
    load_sem, send_sem, recv_sem,
):
    z, x, j = lax.axis_index("dp"), lax.axis_index("row"), lax.axis_index("col")
    c, t = j % 2, j // 2
    o = 1 - c

    barrier = pltpu.get_barrier_semaphore()

    def greet(dev):
        pl.semaphore_signal(barrier, inc=1, device_id=dev, device_id_type=MESH)

    def layer_peer(k):
        x2 = (x + k // 8) % 4
        t2 = (t + k) % 8
        return x2, t2

    loads = [
        pltpu.make_async_copy(s_hbm, s, load_sem.at[LS]),
        pltpu.make_async_copy(b_hbm, b, load_sem.at[LB]),
        pltpu.make_async_copy(
            a_hbm.at[:, pl.ds(pl.multiple_of(j * 128, 128), 128)], a, load_sem.at[LA]
        ),
    ]
    for load in loads:
        load.start()

    greet((z, x, t * 2 + o))
    for k in range(1, 4):
        greet(((z + k) % 4, x, j))

    def greet_layer(k, carry):
        x2, t2 = layer_peer(k)
        greet((z, x2, t2 * 2 + c))
        return carry

    lax.fori_loop(1, 32, greet_layer, 0)

    def send(src, dst, rnd, phase, dev):
        pltpu.make_async_remote_copy(
            src_ref=src,
            dst_ref=dst,
            send_sem=send_sem.at[rnd, phase],
            recv_sem=recv_sem.at[rnd, phase],
            device_id=dev,
            device_id_type=MESH,
        ).start()

    def landed(like, rnd, phase):
        pltpu.make_async_copy(like, like, recv_sem.at[rnd, phase]).wait()

    def left(like, rnd, phase):
        pltpu.make_async_copy(like, like, send_sem.at[rnd, phase]).wait()

    partner = (z, x, t * 2 + o)
    row_iota = lax.broadcasted_iota(jnp.int32, (RANK, RANK), 0)
    col_iota = lax.broadcasted_iota(jnp.int32, (RANK, RANK), 1)
    eye = jnp.where(row_iota == col_iota, 1.0, 0.0).astype(F32)

    def factor_start(rnd):
        work[:, :RANK] = gfull[rnd].reshape(RANK, RANK)
        work[:, RANK:] = eye

    sub = lax.broadcasted_iota(jnp.int32, (8, RANK), 0)
    lane = lax.broadcasted_iota(jnp.int32, (8, RANK), 1)

    def spread(row):
        return jnp.broadcast_to(row, (8, RANK))

    def factor_block(blk, carry):
        r0 = pl.multiple_of(blk * 8, 8)
        gp = work[pl.ds(r0, 8), :RANK]
        ep = work[pl.ds(r0, 8), RANK:]
        diag = pltpu.roll(gp, RANK - r0, 1)
        cols = [jnp.broadcast_to(diag[:, i : i + 1], (8, RANK)) for i in range(8)]
        inv = [jnp.where(sub == i, 1.0, 0.0).astype(F32) for i in range(8)]
        pivots = jnp.ones((8, RANK), F32)
        for i in range(8):
            pivot = spread(cols[i][i : i + 1])
            pivots = jnp.where(sub == i, pivot, pivots)
            if i == 7:
                break
            scale = jnp.where(sub > i, cols[i] * (1.0 / pivot), 0.0)
            for m in range(i + 1, 8):
                cols[m] = cols[m] - scale * spread(cols[m][i : i + 1])
            for m in range(i + 1):
                inv[m] = inv[m] - scale * spread(inv[m][i : i + 1])
        root = lax.rsqrt(pivots)
        root = root * (1.5 - 0.5 * pivots * root * root)
        ug = jnp.zeros((8, RANK), F32)
        ue = jnp.zeros((8, RANK), F32)
        for m in range(8):
            weight = inv[m] * root
            ug = ug + weight * spread(gp[m : m + 1])
            ue = ue + weight * spread(ep[m : m + 1])
        work[pl.ds(r0, 8), RANK:] = ue
        rest = jnp.where(lane >= r0 + 8, ug, 0.0)
        work[...] -= lax.dot_general(
            rest, jnp.concatenate([ug, ue], axis=1), TN, precision=HIGHEST, preferred_element_type=F32
        )
        return carry

    def factor_blocks(lo, hi):
        lax.fori_loop(lo, hi, factor_block, 0)

    loads[0].wait()
    st[...] = s[...].T
    pt[0] = st[pl.ds(pl.multiple_of(x * 32, 32), 32), :].reshape(4, 8, HID)
    gfull[0] = eye.reshape(4, 32, RANK)
    loads[2].wait()
    at[...] = a[...].T
    loads[1].wait()

    pl.semaphore_wait(barrier, 35)

    def one_round(rnd, carry):
        lhs = twice(pt[rnd].reshape(32, HID))
        part = folded(lax.dot_general(lhs, b[...], NT, preferred_element_type=F32))
        for h in range(2):
            for i in range(8):
                ysend[rnd, h, i] = part[h * 16 : h * 16 + 16, i * 128 : i * 128 + 128]
        send(ysend.at[rnd, o], ycore.at[rnd], rnd, YC, partner)
        landed(ycore.at[rnd], rnd, YC)
        yown[rnd] = ysend[rnd, c] + ycore[rnd]

        def reduce_y(k, carry):
            t2 = (t + k) % 8
            send(yown.at[rnd, t2], yrs.at[rnd, t], rnd, YR, (z, x, t2 * 2 + c))
            return carry

        lax.fori_loop(1, 8, reduce_y, 0)
        yrs[rnd, t] = yown[rnd, t]
        factor_start(rnd)
        factor_blocks(0, 6)
        landed(yrs.at[rnd, pl.ds(0, 7)], rnd, YR)
        total = yrs[rnd, 0]
        for i in range(1, 8):
            total = total + yrs[rnd, i]
        mine = x * 8 + t
        yt[rnd, c, mine] = total

        def gather_y(k, carry):
            x2, t2 = layer_peer(k)
            piece = yt.at[rnd, c, mine]
            send(piece, piece, rnd, YG, (z, x2, t2 * 2 + c))
            return carry

        lax.fori_loop(1, 32, gather_y, 0)
        factor_blocks(6, 16)
        linv[rnd] = work[:, RANK:]
        landed(yt.at[rnd, c, pl.ds(0, 31)], rnd, YG)
        send(yt.at[rnd, c], yt.at[rnd, c], rnd, YX, partner)

        def m_half(h):
            for i in range(4):
                for m in range(8):
                    high, low = terms(yt[rnd, h, i * 8 + m])
                    ylhs[i * 16 : i * 16 + 16, m * 128 : m * 128 + 128] = high
                    ylhs[64 + i * 16 : 64 + i * 16 + 16, m * 128 : m * 128 + 128] = low
            half = folded(jnp.dot(ylhs[...], a[...], preferred_element_type=F32))
            for i in range(4):
                mzs[rnd, z, pl.ds(pl.multiple_of(i * 32 + h * 16, 16), 16), :] = half[i * 16 : i * 16 + 16]

        m_half(c)
        landed(yt.at[rnd, o], rnd, YX)
        m_half(o)
        for k in range(1, 4):
            send(mzs.at[rnd, z], mzs.at[rnd, z], rnd, MZ, ((z + k) % 4, x, j))
        landed(mzs.at[rnd, pl.ds(0, 3)], rnd, MZ)
        raw = (mzs[rnd, 0] + mzs[rnd, 1]) + (mzs[rnd, 2] + mzs[rnd, 3])
        mt[rnd] = jnp.dot(linv[rnd], raw, precision=HIGHEST, preferred_element_type=F32)

        def x_half(h):
            rows = [mt[rnd, pl.ds(pl.multiple_of(i * 32 + h * 16, 16), 16), :] for i in range(4)]
            half = folded(jnp.dot(twice(jnp.concatenate(rows, axis=0)), at[...], preferred_element_type=F32))
            for i in range(4):
                for m in range(8):
                    xs[rnd, h, i * 8 + m] = half[i * 16 : i * 16 + 16, m * 128 : m * 128 + 128]

        x_half(o)
        send(xs.at[rnd, o], xcore.at[rnd], rnd, XC, partner)
        gown[rnd] = lax.dot_general(
            mt[rnd, pl.ds(pl.multiple_of(z * 32, 32), 32), :], mt[rnd], NT, precision=HIGHEST, preferred_element_type=F32
        )
        send(gown.at[rnd], gcore.at[rnd], rnd, GC, partner)
        x_half(c)
        landed(xcore.at[rnd], rnd, XC)
        xown[rnd] = xs[rnd, c] + xcore[rnd]

        def reduce_x(k, carry):
            x2, t2 = layer_peer(k)
            send(xown.at[rnd, x2 * 8 + t2], xrs.at[rnd, mine], rnd, XR, (z, x2, t2 * 2 + c))
            return carry

        lax.fori_loop(1, 32, reduce_x, 0)
        xrs[rnd, mine] = xown[rnd, mine]
        landed(gcore.at[rnd], rnd, GC)
        gsum[rnd] = gown[rnd] + gcore[rnd]

        def reduce_g(k, carry):
            t2 = (t + k) % 8
            send(gsum.at[rnd], grs.at[rnd, t], rnd, GR, (z, x, t2 * 2 + c))
            return carry

        lax.fori_loop(1, 8, reduce_g, 0)
        grs[rnd, t] = gsum[rnd]
        landed(xrs.at[rnd, pl.ds(0, 31)], rnd, XR)
        total = xrs[rnd, 0]
        for i in range(1, 32):
            total = total + xrs[rnd, i]
        xt[rnd, c, t] = total

        def gather_x(k, carry):
            t2 = (t + k) % 8
            piece = xt.at[rnd, c, t]
            send(piece, piece, rnd, XG, (z, x, t2 * 2 + c))
            return carry

        lax.fori_loop(1, 8, gather_x, 0)
        landed(grs.at[rnd, pl.ds(0, 7)], rnd, GR)
        total = grs[rnd, 0]
        for i in range(1, 8):
            total = total + grs[rnd, i]
        gpart[rnd] = total
        for k in range(1, 4):
            send(gpart.at[rnd], grx.at[rnd, x], rnd, GX, (z, (x + k) % 4, j))
        grx[rnd, x] = gpart[rnd]
        landed(xt.at[rnd, c, pl.ds(0, 7)], rnd, XG)
        send(xt.at[rnd, c], xt.at[rnd, c], rnd, XX, partner)
        landed(xt.at[rnd, o], rnd, XX)

        for h in range(2):
            for m in range(8):
                high, low = terms(xt[rnd, h, m])
                xlhs[h * 16 : h * 16 + 16, m * 128 : m * 128 + 128] = high
                xlhs[32 + h * 16 : 48 + h * 16, m * 128 : m * 128 + 128] = low
        ps[rnd] = folded(jnp.dot(xlhs[...], b[...], preferred_element_type=F32)).reshape(4, 8, HID)
        for k in range(1, 4):
            z2 = (z + k) % 4
            send(ps.at[rnd, z2], prs.at[rnd, z], rnd, PR, (z2, x, j))
        prs[rnd, z] = ps[rnd, z]
        landed(grx.at[rnd, pl.ds(0, 3)], rnd, GX)
        gfull[rnd + 1, z] = (grx[rnd, 0] + grx[rnd, 1]) + (grx[rnd, 2] + grx[rnd, 3])
        for k in range(1, 4):
            piece = gfull.at[rnd + 1, z]
            send(piece, piece, rnd, GZ, ((z + k) % 4, x, j))
        landed(prs.at[rnd, pl.ds(0, 3)], rnd, PR)
        pt[rnd + 1, z] = (prs[rnd, 0] + prs[rnd, 1]) + (prs[rnd, 2] + prs[rnd, 3])
        for k in range(1, 4):
            piece = pt.at[rnd + 1, z]
            send(piece, piece, rnd, PG, ((z + k) % 4, x, j))
        landed(gfull.at[rnd + 1, pl.ds(0, 3)], rnd, GZ)
        landed(pt.at[rnd + 1, pl.ds(0, 3)], rnd, PG)
        return carry

    lax.fori_loop(0, ROUNDS, one_round, 0)

    cf[x] = pt[ROUNDS]
    mg[c, t] = mt[ROUNDS - 1]
    for k in range(1, 4):
        piece = cf.at[x]
        send(piece, piece, 0, PHASES, (z, (x + k) % 4, j))

    def gather_m(k, carry):
        t2 = (t + k) % 8
        piece = mg.at[c, t]
        send(piece, piece, 1, PHASES, (z, x, t2 * 2 + c))
        return carry

    lax.fori_loop(1, 8, gather_m, 0)
    factor_start(ROUNDS)
    factor_blocks(0, 16)
    linv[ROUNDS] = work[:, RANK:]
    landed(mg.at[c, pl.ds(0, 7)], 1, PHASES)
    send(mg.at[c], mg.at[c], 2, PHASES, partner)
    last = linv[ROUNDS]
    scaled = last * math.sqrt(D)

    def emit_basis(h):
        for i in range(8):
            rows = pl.ds(pl.multiple_of((i * 2 + h) * 128, 128), 128)
            basis_ref[rows, :] = lax.dot_general(
                mg[h, i].T, scaled, NT, precision=HIGHEST, preferred_element_type=F32
            )

    emit_basis(c)
    landed(mg.at[o], 2, PHASES)
    emit_basis(o)
    landed(cf.at[pl.ds(0, 3)], 0, PHASES)
    coef_ref[...] = jnp.dot(last, cf[...].reshape(RANK, HID), precision=HIGHEST, preferred_element_type=F32)

    def drain(rnd, carry):
        left(ycore.at[rnd], rnd, YC)
        left(yrs.at[rnd, pl.ds(0, 7)], rnd, YR)
        left(yt.at[rnd, 0, pl.ds(0, 31)], rnd, YG)
        left(yt.at[rnd, 0], rnd, YX)
        left(mzs.at[rnd, pl.ds(0, 3)], rnd, MZ)
        left(xcore.at[rnd], rnd, XC)
        left(xrs.at[rnd, pl.ds(0, 31)], rnd, XR)
        left(xt.at[rnd, 0, pl.ds(0, 7)], rnd, XG)
        left(xt.at[rnd, 0], rnd, XX)
        left(prs.at[rnd, pl.ds(0, 3)], rnd, PR)
        left(pt.at[rnd, pl.ds(0, 3)], rnd, PG)
        left(gcore.at[rnd], rnd, GC)
        left(grs.at[rnd, pl.ds(0, 7)], rnd, GR)
        left(grx.at[rnd, pl.ds(0, 3)], rnd, GX)
        left(gfull.at[rnd, pl.ds(0, 3)], rnd, GZ)
        return carry

    lax.fori_loop(0, ROUNDS, drain, 0)
    left(cf.at[pl.ds(0, 3)], 0, PHASES)
    left(mg.at[0, pl.ds(0, 7)], 1, PHASES)
    left(mg.at[0], 2, PHASES)


def body(activations, grad_out, sketch):
    anywhere = pl.BlockSpec(memory_space=pl.ANY)
    inside = pl.BlockSpec(memory_space=pltpu.VMEM)
    vm = pltpu.VMEM
    n = ROUNDS
    return pl.pallas_call(
        kernel,
        name="range_finder",
        out_shape=(
            jax.ShapeDtypeStruct((2048, RANK), F32),
            jax.ShapeDtypeStruct((RANK, HID), F32),
        ),
        in_specs=[anywhere] * 3,
        out_specs=(inside, inside),
        scratch_shapes=[
            vm((TOK, 128), BF16),
            vm((128, TOK), BF16),
            vm((TOK, HID), BF16),
            vm((HID, RANK), F32),
            vm((RANK, HID), F32),
            vm((n + 1, 4, 8, HID), F32),
            vm((n, 2, 8, 16, 128), F32),
            vm((n, 8, 16, 128), F32),
            vm((n, 8, 16, 128), F32),
            vm((n, 8, 16, 128), F32),
            vm((n, 2, 32, 16, 128), F32),
            vm((128, TOK), BF16),
            vm((n, 4, RANK, 128), F32),
            vm((n, RANK, 128), F32),
            vm((n, 2, 32, 16, 128), F32),
            vm((n, 32, 16, 128), F32),
            vm((n, 32, 16, 128), F32),
            vm((n, 32, 16, 128), F32),
            vm((n, 2, 8, 16, 128), F32),
            vm((64, TOK), BF16),
            vm((n, 4, 8, HID), F32),
            vm((n, 4, 8, HID), F32),
            vm((n, 32, RANK), F32),
            vm((n, 32, RANK), F32),
            vm((n, 32, RANK), F32),
            vm((n, 8, 32, RANK), F32),
            vm((n, 32, RANK), F32),
            vm((n, 4, 32, RANK), F32),
            vm((n + 1, 4, 32, RANK), F32),
            vm((RANK, 2 * RANK), F32),
            vm((n + 1, RANK, RANK), F32),
            vm((4, 4, 8, HID), F32),
            vm((2, 8, RANK, 128), F32),
            pltpu.SemaphoreType.DMA((3,)),
            pltpu.SemaphoreType.DMA((n, PHASES + 1)),
            pltpu.SemaphoreType.DMA((n, PHASES + 1)),
        ],
        compiler_params=pltpu.CompilerParams(
            collective_id=0, has_side_effects=True, vmem_limit_bytes=48 * 2**20
        ),
    )(activations, grad_out, sketch)


def solution(mesh):
    in_specs = (P("dp", "row"), P("dp", "col"), P("col", None))
    out_specs = (P("row", None), P(None, "col"))
    return jax.shard_map(body, mesh=mesh, in_specs=in_specs, out_specs=out_specs, check_vma=False)
```

time: 1890 us -> 221 us (0.12)
  waiting for transfers between devices: 1710 us -> 0 us
  Pallas kernels: 0 us -> 212 us
  other arithmetic: 73.5 us -> 0 us
  matrix products: 63 us -> 0 us
    psum x9 -> x0, waiting for transfers between devices: 1440 us -> none  [the longest x3 546 us: range_basis(): rows_part = lax.psum(jnp.dot(piece, mat, precision=hp), 'col')]
    reduce_scatter x1 -> x0, waiting for transfers between devices: 238 us -> none  [body(): lax.psum_scatter(jnp.einsum('tk,tf->kf', activations, grad_out, preferred...]
    pallas_call x0 -> x1, Pallas kernels: none -> 212 us  [body(): pl.pallas_call(kernel, name='range_finder', out_shape=(jax.ShapeDtypeStru...]
    another operation x15 -> x0, other arithmetic: 68.6 us -> none  [the longest x9 37.2 us: cholesky_basis(): lower = jnp.linalg.cholesky(gram)]
    dot_general x10 -> x0, matrix products: 58.2 us -> none  [the longest x3 17.3 us: range_basis(): rows_part = lax.psum(jnp.dot(piece, mat, precision=hp), 'col')]
    all_gather x1 -> x0, waiting for transfers between devices: 34.3 us -> none  [body(): basis = lax.all_gather(basis_part, 'dp', axis=0, tiled=True)]
  transfers between devices with their start and end apart: 11 -> 0, of which waited for: 11 -> 0; matrix products, arithmetic and copies ran while one was open for 1% -> 0% of each run, Pallas kernels for 0% -> 0%
where the time goes in v2:
time: 221 us; the launch traced here: 217 us
  Pallas kernels  212 us (96%)
  local copies, waits for them, and re-layouts  4.99 us (2%)
    pallas_call x1, Pallas kernels, body(): pl.pallas_call(kernel, name='range_finder', out_shape=(jax.ShapeDtypeStru...  212 us
    unnamed x6, local copies, waits for them, and re-layouts  4.99 us

profile of v2, /device:TPU:1, one launch (start us, length us, event | category | flops | bytes accessed | tf_op | source)
XLA Modules:
  0.0 217.3 jit_solution(8767096167327615681)
XLA Ops:
  0.6 0.0 copy-start
  0.6 2.0 copy-done
  2.6 0.0 copy-start.1
  2.6 1.2 copy-done.1
  3.8 211.7 %range_finder.1 = (f32[2048,128]{1,0:T(8,128)S(1)}, f32[128,1664]{1,0:T(8,128)S(1)}) custom-call(bf16[1024,2048]{1,0:T(8,128)(2,1)} %a_hbm.1, bf16[1024,1664]{1,0:T(8,128)(2,1)S(1)} %copy-done, f32[1664,128]{1,0:T(8,128)S(1)} %copy-done.1), custom_call_target="tpu_custom_call" | custom-call | tf_op jit(solution)/shard_map/range_finder/pallas_call | solution.py:366
  215.4 1.0 copy.7
  216.4 0.9 copy.8
Async XLA Ops:
  0.6 2.0 copy-start
  2.6 1.2 copy-start.1

commit v3 on v0

v3 whole, which is shorter than its diff:
```python
import functools
import math

import jax
import jax.numpy as jnp
from jax import lax
from jax.experimental import pallas as pl
from jax.experimental.pallas import tpu as pltpu
from jax.sharding import PartitionSpec as P

MESH = pl.DeviceIdType.MESH
F32 = jnp.float32
BF16 = jnp.bfloat16
HIGHEST = lax.Precision.HIGHEST
D = 8192
RANK = 128
ROUNDS = 3
TOK = 1024
HID = 1664
FEAT = 512
NT = (((1,), (1,)), ((), ()))
TN = (((0,), (0,)), ((), ()))
PARTS = ((0, 896), (896, 768))
YC, YR, YG, MR, MG, MC, XR, XG, XC, PRA, PRB, PGA, PGB, GY, GX, GZ = range(16)
PR, PG = (PRA, PRB), (PGA, PGB)
PHASES = 16
HY = ((1, 2), (1, 1), (1, 3), (1, 0), (0, 2), (0, 1), (0, 3))
XY = (
    (2, 2), (2, 1), (2, 3), (1, 2), (3, 2), (1, 1), (1, 3), (3, 1), (3, 3),
    (2, 0), (0, 2), (1, 0), (3, 0), (0, 1), (0, 3),
)
ZH = ((2, 1), (1, 1), (3, 1), (0, 1), (2, 0), (1, 0), (3, 0))


def stacked(mat):
    high = mat.astype(BF16)
    rest = mat - high.astype(F32)
    mid = rest.astype(BF16)
    low = (rest - mid.astype(F32)).astype(BF16)
    return jnp.concatenate([high, mid, low], axis=0)


def folded(wide):
    rows = wide.shape[0] // 3
    return wide[:rows] + (wide[rows : 2 * rows] + wide[2 * rows :])


def kernel(
    a_hbm, b_hbm, s_hbm, basis_ref, coef_ref,
    a, b, s, st, pt, ysend, ycore, yown, yrs, yt, ms, mrs, mraw, mfull, mt, xs, xrs, xt,
    ps, prs, gown, gys, gsum, gxs, gfull, work, linv, cf, mg,
    load_sem, send_sem, recv_sem,
):
    z, x, j = lax.axis_index("dp"), lax.axis_index("row"), lax.axis_index("col")
    c = j % 2
    y = (j // 2) % 4
    h = j // 8
    o = 1 - c
    mine_hy = h * 4 + y
    mine_xy = x * 4 + y
    mine_hz = h * 4 + z

    def dev(z_, x_, h_, y_, c_):
        return (z_, x_, (h_ * 4 + y_) * 2 + c_)

    partner = dev(z, x, h, y, o)
    hy_peers = [((h + dh) % 2, (y + dy) % 4) for dh, dy in HY]
    xy_peers = [((x + dx) % 4, (y + dy) % 4) for dx, dy in XY]
    zh_peers = [((z + dz) % 4, (h + dh) % 2) for dz, dh in ZH]
    z_peers = [(z + k) % 4 for k in (2, 1, 3)]
    y_peers = [(y + k) % 4 for k in (2, 1, 3)]
    x_peers = [(x + k) % 4 for k in (2, 1, 3)]

    barrier = pltpu.get_barrier_semaphore()

    def greet(device):
        pl.semaphore_signal(barrier, inc=1, device_id=device, device_id_type=MESH)

    loads = [
        pltpu.make_async_copy(s_hbm, s, load_sem.at[0]),
        pltpu.make_async_copy(b_hbm, b, load_sem.at[1]),
        pltpu.make_async_copy(
            a_hbm.at[:, pl.ds(pl.multiple_of(y * FEAT, FEAT), FEAT)], a, load_sem.at[2]
        ),
    ]
    for load in loads:
        load.start()

    for h2, y2 in hy_peers:
        greet(dev(z, x, h2, y2, c))
    for (x2, y2), (dx, _) in zip(xy_peers, XY):
        if dx:
            greet(dev(z, x2, h, y2, c))
    for (z2, h2), (dz, _) in zip(zh_peers, ZH):
        if dz:
            greet(dev(z2, x, h2, y, c))
    greet(partner)

    def send(src, dst, rnd, phase, device):
        pltpu.make_async_remote_copy(
            src_ref=src,
            dst_ref=dst,
            send_sem=send_sem.at[rnd, phase],
            recv_sem=recv_sem.at[rnd, phase],
            device_id=device,
            device_id_type=MESH,
        ).start()

    def landed(like, rnd, phase):
        pltpu.make_async_copy(like, like, recv_sem.at[rnd, phase]).wait()

    def left(like, rnd, phase):
        pltpu.make_async_copy(like, like, send_sem.at[rnd, phase]).wait()

    row_iota = lax.broadcasted_iota(jnp.int32, (RANK, RANK), 0)
    col_iota = lax.broadcasted_iota(jnp.int32, (RANK, RANK), 1)
    eye = jnp.where(row_iota == col_iota, 1.0, 0.0).astype(F32)

    def factor_start(rnd):
        work[:, :RANK] = gfull[rnd].reshape(RANK, RANK)
        work[:, RANK:] = eye

    sub = lax.broadcasted_iota(jnp.int32, (8, RANK), 0)
    lane = lax.broadcasted_iota(jnp.int32, (8, RANK), 1)

    def spread(row):
        return jnp.broadcast_to(row, (8, RANK))

    def factor_block(blk, carry):
        r0 = pl.multiple_of(blk * 8, 8)
        gp = work[pl.ds(r0, 8), :RANK]
        ep = work[pl.ds(r0, 8), RANK:]
        diag = pltpu.roll(gp, RANK - r0, 1)
        cols = [jnp.broadcast_to(diag[:, i : i + 1], (8, RANK)) for i in range(8)]
        inv = [jnp.where(sub == i, 1.0, 0.0).astype(F32) for i in range(8)]
        pivots = jnp.ones((8, RANK), F32)
        for i in range(8):
            pivot = spread(cols[i][i : i + 1])
            pivots = jnp.where(sub == i, pivot, pivots)
            if i == 7:
                break
            scale = jnp.where(sub > i, cols[i] * (1.0 / pivot), 0.0)
            for m in range(i + 1, 8):
                cols[m] = cols[m] - scale * spread(cols[m][i : i + 1])
            for m in range(i + 1):
                inv[m] = inv[m] - scale * spread(inv[m][i : i + 1])
        root = lax.rsqrt(pivots)
        root = root * (1.5 - 0.5 * pivots * root * root)
        ug = jnp.zeros((8, RANK), F32)
        ue = jnp.zeros((8, RANK), F32)
        for m in range(8):
            weight = inv[m] * root
            ug = ug + weight * spread(gp[m : m + 1])
            ue = ue + weight * spread(ep[m : m + 1])
        work[pl.ds(r0, 8), RANK:] = ue
        rest = jnp.where(lane >= r0 + 8, ug, 0.0)
        work[...] -= lax.dot_general(
            rest, jnp.concatenate([ug, ue], axis=1), TN, precision=HIGHEST, preferred_element_type=F32
        )
        return carry

    def factor_blocks(lo, hi):
        lax.fori_loop(lo, hi, factor_block, 0)

    def tokens_part(rnd):
        lhs = stacked(pt[rnd].reshape(32, HID))
        part = folded(lax.dot_general(lhs, b[...], NT, preferred_element_type=F32))
        for i in range(4):
            for m in range(4):
                ysend[rnd, i // 2, (i % 2) * 4 + m] = part[i * 8 : i * 8 + 8, m * 256 : m * 256 + 256]

    loads[0].wait()
    st[...] = s[...].T
    pt[0] = st[pl.ds(pl.multiple_of(x * 32, 32), 32), :].reshape(4, 8, HID)
    work[:, :RANK] = eye
    work[:, RANK:] = eye
    loads[1].wait()
    tokens_part(0)
    loads[2].wait()

    pl.semaphore_wait(barrier, 26)

    def one_round(rnd, carry):
        send(ysend.at[rnd, o], ycore.at[rnd], rnd, YC, partner)
        landed(ycore.at[rnd], rnd, YC)
        yown[rnd] = ysend[rnd, c] + ycore[rnd]
        for h2, y2 in hy_peers:
            send(yown.at[rnd, h2 * 4 + y2], yrs.at[rnd, mine_hy], rnd, YR, dev(z, x, h2, y2, c))
        yrs[rnd, mine_hy] = yown[rnd, mine_hy]
        factor_blocks(6, 12)
        landed(yrs.at[rnd, pl.ds(0, 7)], rnd, YR)
        total = yrs[rnd, 0]
        for i in range(1, 8):
            total = total + yrs[rnd, i]
        yt[rnd, mine_xy] = total
        for x2, y2 in xy_peers:
            piece = yt.at[rnd, mine_xy]
            send(piece, piece, rnd, YG, dev(z, x2, h, y2, c))
        factor_blocks(12, 16)
        linv[rnd] = work[:, RANK:]
        landed(yt.at[rnd, pl.ds(0, 15)], rnd, YG)

        rows = [jnp.concatenate([yt[rnd, i * 4 + m] for m in range(4)], axis=1) for i in range(4)]
        lhs = stacked(jnp.concatenate(rows, axis=0))
        part = folded(jnp.dot(lhs, a[...], preferred_element_type=F32))
        for i in range(4):
            ms[rnd, i] = part[:, i * 128 : i * 128 + 128]
        for z2 in z_peers:
            send(ms.at[rnd, z2], mrs.at[rnd, z], rnd, MR, dev(z2, x, h, y, c))
        mrs[rnd, z] = ms[rnd, z]
        landed(mrs.at[rnd, pl.ds(0, 3)], rnd, MR)
        mraw[rnd, c, mine_hz] = (mrs[rnd, 0] + mrs[rnd, 1]) + (mrs[rnd, 2] + mrs[rnd, 3])
        for z2, h2 in zh_peers:
            piece = mraw.at[rnd, c, mine_hz]
            send(piece, piece, rnd, MG, dev(z2, x, h2, y, c))
        landed(mraw.at[rnd, c, pl.ds(0, 7)], rnd, MG)
        send(mraw.at[rnd, c], mraw.at[rnd, c], rnd, MC, partner)
        landed(mraw.at[rnd, o], rnd, MC)
        for cc in range(2):
            for hh in range(2):
                for zz in range(4):
                    for i in range(4):
                        r0 = i * 32 + cc * 16 + hh * 8
                        mfull[r0 : r0 + 8, zz * 128 : zz * 128 + 128] = mraw[
                            rnd, cc, hh * 4 + zz, i * 8 : i * 8 + 8, :
                        ]
        mt[rnd] = jnp.dot(linv[rnd], mfull[...], precision=HIGHEST, preferred_element_type=F32)

        rows = [mt[rnd, pl.ds(pl.multiple_of(i * 32 + c * 16 + h * 8, 8), 8), :] for i in range(4)]
        lhs = stacked(jnp.concatenate(rows, axis=0))
        part = folded(lax.dot_general(lhs, a[...], NT, preferred_element_type=F32))
        for i in range(4):
            for m in range(4):
                xs[rnd, i * 4 + m] = part[i * 8 : i * 8 + 8, m * 256 : m * 256 + 256]
        for x2, y2 in xy_peers:
            send(xs.at[rnd, x2 * 4 + y2], xrs.at[rnd, mine_xy], rnd, XR, dev(z, x2, h, y2, c))
        xrs[rnd, mine_xy] = xs[rnd, mine_xy]
        gown[rnd] = lax.dot_general(
            mt[rnd, pl.ds(pl.multiple_of(z * 32, 32), 32), :], mt[rnd], NT, precision=HIGHEST, preferred_element_type=F32
        )
        for y2 in y_peers:
            send(gown.at[rnd], gys.at[rnd, y], rnd, GY, dev(z, x, h, y2, c))
        gys[rnd, y] = gown[rnd]
        landed(xrs.at[rnd, pl.ds(0, 15)], rnd, XR)
        total = xrs[rnd, 0]
        for i in range(1, 16):
            total = total + xrs[rnd, i]
        xt[rnd, c, mine_hy] = total
        for h2, y2 in hy_peers:
            piece = xt.at[rnd, c, mine_hy]
            send(piece, piece, rnd, XG, dev(z, x, h2, y2, c))
        landed(gys.at[rnd, pl.ds(0, 3)], rnd, GY)
        gsum[rnd] = (gys[rnd, 0] + gys[rnd, 1]) + (gys[rnd, 2] + gys[rnd, 3])
        for x2 in x_peers:
            send(gsum.at[rnd], gxs.at[rnd, x], rnd, GX, dev(z, x2, h, y, c))
        gxs[rnd, x] = gsum[rnd]

        landed(xt.at[rnd, c, pl.ds(0, 7)], rnd, XG)
        send(xt.at[rnd, c], xt.at[rnd, c], rnd, XC, partner)

        @pl.when(rnd == ROUNDS - 1)
        def _():
            for y2 in y_peers:
                send(
                    mt.at[rnd, :, pl.ds(pl.multiple_of(c * 256, 256), 256)],
                    mg.at[y, c],
                    0, PHASES,
                    dev(z, x, h, y2, c),
                )

        landed(xt.at[rnd, o], rnd, XC)

        rows = [jnp.concatenate([xt[rnd, i // 2, (i % 2) * 4 + m] for m in range(4)], axis=1) for i in range(4)]
        lhs = stacked(jnp.concatenate(rows, axis=0))
        for n, (lo, size) in enumerate(PARTS):
            part = folded(jnp.dot(lhs, b[:, lo : lo + size], preferred_element_type=F32))
            ps[rnd, :, :, lo : lo + size] = part.reshape(4, 8, size)
            for z2 in z_peers:
                span = pl.ds(lo, size)
                send(ps.at[rnd, z2, :, span], prs.at[rnd, z, :, span], rnd, PR[n], dev(z2, x, h, y, c))
        prs[rnd, z] = ps[rnd, z]
        landed(gxs.at[rnd, pl.ds(0, 3)], rnd, GX)
        gfull[rnd, z] = (gxs[rnd, 0] + gxs[rnd, 1]) + (gxs[rnd, 2] + gxs[rnd, 3])
        for z2 in z_peers:
            piece = gfull.at[rnd, z]
            send(piece, piece, rnd, GZ, dev(z2, x, h, y, c))
        for n, (lo, size) in enumerate(PARTS):
            span = pl.ds(lo, size)
            landed(prs.at[rnd, pl.ds(0, 3), :, span], rnd, PR[n])
            got = [prs[rnd, i, :, lo : lo + size] for i in range(4)]
            pt[rnd + 1, z, :, lo : lo + size] = (got[0] + got[1]) + (got[2] + got[3])
            for z2 in z_peers:
                piece = pt.at[rnd + 1, z, :, span]
                send(piece, piece, rnd, PG[n], dev(z2, x, h, y, c))
        landed(gfull.at[rnd, pl.ds(0, 3)], rnd, GZ)
        factor_start(rnd)
        factor_blocks(0, 6)

        @pl.when(rnd < ROUNDS - 1)
        def _():
            for n, (lo, size) in enumerate(PARTS):
                landed(pt.at[rnd + 1, pl.ds(0, 3), :, pl.ds(lo, size)], rnd, PG[n])
            tokens_part(rnd + 1)

        return carry

    lax.fori_loop(0, ROUNDS, one_round, 0)

    last = ROUNDS - 1
    for x2 in x_peers:
        send(pt.at[ROUNDS, z], cf.at[x, z], 2, PHASES, dev(z, x2, h, y, c))
    for n, (lo, size) in enumerate(PARTS):
        landed(pt.at[ROUNDS, pl.ds(0, 3), :, pl.ds(lo, size)], last, PG[n])
    for z2 in z_peers:
        for x2 in x_peers:
            send(pt.at[ROUNDS, z2], cf.at[x, z2], 2, PHASES, dev(z, x2, h, y, c))
    landed(mg.at[pl.ds(0, 3), 0], 0, PHASES)
    for y2 in y_peers:
        piece = mg.at[y2, c]
        send(piece, piece, 1, PHASES, partner)
    for cc in range(2):
        mg[y, cc] = mt[last, :, cc * 256 : cc * 256 + 256]
    cf[x] = pt[ROUNDS]
    factor_blocks(6, 16)
    final = work[:, RANK:]
    scaled = final * math.sqrt(D)
    landed(mg.at[pl.ds(0, 3), 0], 1, PHASES)
    for i in range(4):
        for cc in range(2):
            r0 = i * FEAT + cc * 256
            basis_ref[r0 : r0 + 256, :] = lax.dot_general(
                mg[i, cc].T, scaled, NT, precision=HIGHEST, preferred_element_type=F32
            )
    landed(cf.at[pl.ds(0, 3)], 2, PHASES)
    coef_ref[...] = jnp.dot(final, cf[...].reshape(RANK, HID), precision=HIGHEST, preferred_element_type=F32)

    def drain(rnd, carry):
        left(ycore.at[rnd], rnd, YC)
        left(yrs.at[rnd, pl.ds(0, 7)], rnd, YR)
        left(yt.at[rnd, pl.ds(0, 15)], rnd, YG)
        left(mrs.at[rnd, pl.ds(0, 3)], rnd, MR)
        left(mraw.at[rnd, 0, pl.ds(0, 7)], rnd, MG)
        left(mraw.at[rnd, 0], rnd, MC)
        left(xrs.at[rnd, pl.ds(0, 15)], rnd, XR)
        left(xt.at[rnd, 0, pl.ds(0, 7)], rnd, XG)
        left(xt.at[rnd, 0], rnd, XC)
        for n, (lo, size) in enumerate(PARTS):
            span = pl.ds(lo, size)
            left(prs.at[rnd, pl.ds(0, 3), :, span], rnd, PR[n])
            left(pt.at[rnd, pl.ds(0, 3), :, span], rnd, PG[n])
        left(gys.at[rnd, pl.ds(0, 3)], rnd, GY)
        left(gxs.at[rnd, pl.ds(0, 3)], rnd, GX)
        left(gfull.at[rnd, pl.ds(0, 3)], rnd, GZ)
        return carry

    lax.fori_loop(0, ROUNDS, drain, 0)
    left(mg.at[pl.ds(0, 3), 0], 0, PHASES)
    left(mg.at[pl.ds(0, 3), 0], 1, PHASES)
    left(cf.at[pl.ds(0, 3)], 2, PHASES)


def body(activations, grad_out, sketch):
    anywhere = pl.BlockSpec(memory_space=pl.ANY)
    inside = pl.BlockSpec(memory_space=pltpu.VMEM)
    vm = pltpu.VMEM
    n = ROUNDS
    return pl.pallas_call(
        kernel,
        name="range_finder",
        out_shape=(
            jax.ShapeDtypeStruct((2048, RANK), F32),
            jax.ShapeDtypeStruct((RANK, HID), F32),
        ),
        in_specs=[anywhere] * 3,
        out_specs=(inside, inside),
        scratch_shapes=[
            vm((TOK, FEAT), BF16),
            vm((TOK, HID), BF16),
            vm((HID, RANK), F32),
            vm((RANK, HID), F32),
            vm((n + 1, 4, 8, HID), F32),
            vm((n, 2, 8, 8, 256), F32),
            vm((n, 8, 8, 256), F32),
            vm((n, 8, 8, 256), F32),
            vm((n, 8, 8, 256), F32),
            vm((n, 16, 8, 256), F32),
            vm((n, 4, 32, 128), F32),
            vm((n, 4, 32, 128), F32),
            vm((n, 2, 8, 32, 128), F32),
            vm((RANK, FEAT), F32),
            vm((n, RANK, FEAT), F32),
            vm((n, 16, 8, 256), F32),
            vm((n, 16, 8, 256), F32),
            vm((n, 2, 8, 8, 256), F32),
            vm((n, 4, 8, HID), F32),
            vm((n, 4, 8, HID), F32),
            vm((n, 32, RANK), F32),
            vm((n, 4, 32, RANK), F32),
            vm((n, 32, RANK), F32),
            vm((n, 4, 32, RANK), F32),
            vm((n, 4, 32, RANK), F32),
            vm((RANK, 2 * RANK), F32),
            vm((n, RANK, RANK), F32),
            vm((4, 4, 8, HID), F32),
            vm((4, 2, RANK, 256), F32),
            pltpu.SemaphoreType.DMA((3,)),
            pltpu.SemaphoreType.DMA((n, PHASES + 1)),
            pltpu.SemaphoreType.DMA((n, PHASES + 1)),
        ],
        compiler_params=pltpu.CompilerParams(
            collective_id=0, has_side_effects=True, vmem_limit_bytes=48 * 2**20
        ),
    )(activations, grad_out, sketch)


def solution(mesh):
    in_specs = (P("dp", "row"), P("dp", "col"), P("col", None))
    out_specs = (P("row", None), P(None, "col"))
    return jax.shard_map(body, mesh=mesh, in_specs=in_specs, out_specs=out_specs, check_vma=False)
```

time: 1890 us -> 173 us (0.09); the launches traced: 1870 us -> 173 us
  waiting for transfers between devices: 1710 us -> 0 us
  Pallas kernels: 0 us -> 168 us
  other arithmetic: 73.5 us -> 0 us
  matrix products: 63 us -> 0 us
    psum x9 -> x0, waiting for transfers between devices: 1440 us -> none  [the longest x3 546 us: range_basis(): rows_part = lax.psum(jnp.dot(piece, mat, precision=hp), 'col')]
    reduce_scatter x1 -> x0, waiting for transfers between devices: 238 us -> none  [body(): lax.psum_scatter(jnp.einsum('tk,tf->kf', activations, grad_out, preferred...]
    pallas_call x0 -> x1, Pallas kernels: none -> 168 us  [body(): pl.pallas_call(kernel, name='range_finder', out_shape=(jax.ShapeDtypeStru...]
    another operation x15 -> x0, other arithmetic: 68.6 us -> none  [the longest x9 37.2 us: cholesky_basis(): lower = jnp.linalg.cholesky(gram)]
    dot_general x10 -> x0, matrix products: 58.2 us -> none  [the longest x3 17.3 us: range_basis(): rows_part = lax.psum(jnp.dot(piece, mat, precision=hp), 'col')]
    all_gather x1 -> x0, waiting for transfers between devices: 34.3 us -> none  [body(): basis = lax.all_gather(basis_part, 'dp', axis=0, tiled=True)]
  transfers between devices with their start and end apart: 11 -> 0, of which waited for: 11 -> 0; matrix products, arithmetic and copies ran while one was open for 1% -> 0% of each run, Pallas kernels for 0% -> 0%
where the time goes in v3:
time: 173 us
  Pallas kernels  168 us (97%)
  local copies, waits for them, and re-layouts  4.99 us (3%)
    pallas_call x1, Pallas kernels, body(): pl.pallas_call(kernel, name='range_finder', out_shape=(jax.ShapeDtypeStru...  168 us
    unnamed x6, local copies, waits for them, and re-layouts  4.99 us

profile of v3, /device:TPU:1, one launch (start us, length us, event | category | flops | bytes accessed | tf_op | source)
XLA Modules:
  0.0 173.3 jit_solution(7088876419582323741)
XLA Ops:
  0.6 0.0 copy-start
  0.6 2.0 %copy-done = bf16[1024,1664]{1,0:T(8,128)(2,1)S(1)} copy-done((bf16[1024,1664]{1,0:T(8,128)(2,1)S(1)}, bf16[1024,1664]{1,0:T(8,128)(2,1)}, u32[]{:S(2)}) %copy-start) | copy-done | bytes 3407896
  2.6 0.0 copy-start.1
  2.6 1.2 copy-done.1
  3.8 167.7 %range_finder.1 = (f32[2048,128]{1,0:T(8,128)S(1)}, f32[128,1664]{1,0:T(8,128)S(1)}) custom-call(bf16[1024,2048]{1,0:T(8,128)(2,1)} %a_hbm.1, bf16[1024,1664]{1,0:T(8,128)(2,1)S(1)} %copy-done, f32[1664,128]{1,0:T(8,128)S(1)} %copy-done.1), custom_call_target="tpu_custom_call" | custom-call | tf_op jit(solution)/shard_map/range_finder/pallas_call | solution.py:367
  171.4 1.0 copy.7
  172.4 0.9 copy.8
Async XLA Ops:
  0.6 2.0 %copy-start = (bf16[1024,1664]{1,0:T(8,128)(2,1)S(1)}, bf16[1024,1664]{1,0:T(8,128)(2,1)}, u32[]{:S(2)}) copy-start(bf16[1024,1664]{1,0:T(8,128)(2,1)} %b_hbm.1) | copy-start | bytes 10223620
  2.6 1.2 copy-start.1

commit v4 on v3

--- a/solution.py
+++ b/solution.py
@@ -21,10 +21,10 @@
 NT = (((1,), (1,)), ((), ()))
 TN = (((0,), (0,)), ((), ()))
 PARTS = ((0, 896), (896, 768))
-YC, YR, YG, MR, MG, MC, XR, XG, XC, PRA, PRB, PGA, PGB, GY, GX, GZ = range(16)
-PR, PG = (PRA, PRB), (PGA, PGB)
-PHASES = 16
-HY = ((1, 2), (1, 1), (1, 3), (1, 0), (0, 2), (0, 1), (0, 3))
+YC, YR, YG, MRA, MRB, MGA, MGB, MC, XR, XG, XC, PRA, PRB, GY, GX, GZ, GC = range(17)
+MR, MG, PR = (MRA, MRB), (MGA, MGB), (PRA, PRB)
+PG = (17, 21)
+PHASES = 25
 XY = (
     (2, 2), (2, 1), (2, 3), (1, 2), (3, 2), (1, 1), (1, 3), (3, 1), (3, 3),
     (2, 0), (0, 2), (1, 0), (3, 0), (0, 1), (0, 3),
@@ -47,7 +47,7 @@
 
 def kernel(
     a_hbm, b_hbm, s_hbm, basis_ref, coef_ref,
-    a, b, s, st, pt, ysend, ycore, yown, yrs, yt, ms, mrs, mraw, mfull, mt, xs, xrs, xt,
+    a, b, s, st, pt, ysend, ycore, yown, yrs, yt, ms, mrs, mraw, mfull, mt, xl, xs, xrs, xt,
     ps, prs, gown, gys, gsum, gxs, gfull, work, linv, cf, mg,
     load_sem, send_sem, recv_sem,
 ):
@@ -56,7 +56,6 @@
     y = (j // 2) % 4
     h = j // 8
     o = 1 - c
-    mine_hy = h * 4 + y
     mine_xy = x * 4 + y
     mine_hz = h * 4 + z
 
@@ -64,7 +63,6 @@
         return (z_, x_, (h_ * 4 + y_) * 2 + c_)
 
     partner = dev(z, x, h, y, o)
-    hy_peers = [((h + dh) % 2, (y + dy) % 4) for dh, dy in HY]
     xy_peers = [((x + dx) % 4, (y + dy) % 4) for dx, dy in XY]
     zh_peers = [((z + dz) % 4, (h + dh) % 2) for dz, dh in ZH]
     z_peers = [(z + k) % 4 for k in (2, 1, 3)]
@@ -86,14 +84,10 @@
     for load in loads:
         load.start()
 
-    for h2, y2 in hy_peers:
-        greet(dev(z, x, h2, y2, c))
-    for (x2, y2), (dx, _) in zip(xy_peers, XY):
-        if dx:
-            greet(dev(z, x2, h, y2, c))
-    for (z2, h2), (dz, _) in zip(zh_peers, ZH):
-        if dz:
-            greet(dev(z2, x, h2, y, c))
+    for x2, y2 in xy_peers:
+        greet(dev(z, x2, h, y2, c))
+    for z2, h2 in zh_peers:
+        greet(dev(z2, x, h2, y, c))
     greet(partner)
 
     def send(src, dst, rnd, phase, device):
@@ -165,9 +159,9 @@
     def tokens_part(rnd):
         lhs = stacked(pt[rnd].reshape(32, HID))
         part = folded(lax.dot_general(lhs, b[...], NT, preferred_element_type=F32))
-        for i in range(4):
+        for i in range(2):
             for m in range(4):
-                ysend[rnd, i // 2, (i % 2) * 4 + m] = part[i * 8 : i * 8 + 8, m * 256 : m * 256 + 256]
+                ysend[rnd, i, m] = part[i * 16 : i * 16 + 16, m * 256 : m * 256 + 256]
 
     loads[0].wait()
     st[...] = s[...].T
@@ -178,65 +172,91 @@
     tokens_part(0)
     loads[2].wait()
 
-    pl.semaphore_wait(barrier, 26)
+    pl.semaphore_wait(barrier, 23)
+
+    def gathered_p(rnd, z2):
+        for n, (lo, size) in enumerate(PARTS):
+            landed(pt.at[rnd + 1, z2, :, pl.ds(lo, size)], rnd, PG[n] + z2)
 
     def one_round(rnd, carry):
         send(ysend.at[rnd, o], ycore.at[rnd], rnd, YC, partner)
         landed(ycore.at[rnd], rnd, YC)
         yown[rnd] = ysend[rnd, c] + ycore[rnd]
-        for h2, y2 in hy_peers:
-            send(yown.at[rnd, h2 * 4 + y2], yrs.at[rnd, mine_hy], rnd, YR, dev(z, x, h2, y2, c))
-        yrs[rnd, mine_hy] = yown[rnd, mine_hy]
-        factor_blocks(6, 12)
-        landed(yrs.at[rnd, pl.ds(0, 7)], rnd, YR)
-        total = yrs[rnd, 0]
-        for i in range(1, 8):
-            total = total + yrs[rnd, i]
-        yt[rnd, mine_xy] = total
+        for y2 in y_peers:
+            send(yown.at[rnd, y2], yrs.at[rnd, y], rnd, YR, dev(z, x, h, y2, c))
+        yrs[rnd, y] = yown[rnd, y]
+        factor_blocks(6, 9)
+        landed(yrs.at[rnd, pl.ds(0, 3)], rnd, YR)
+        yt[rnd, mine_xy] = (yrs[rnd, 0] + yrs[rnd, 1]) + (yrs[rnd, 2] + yrs[rnd, 3])
         for x2, y2 in xy_peers:
             piece = yt.at[rnd, mine_xy]
             send(piece, piece, rnd, YG, dev(z, x2, h, y2, c))
-        factor_blocks(12, 16)
-        linv[rnd] = work[:, RANK:]
+        factor_blocks(9, 15)
         landed(yt.at[rnd, pl.ds(0, 15)], rnd, YG)
 
         rows = [jnp.concatenate([yt[rnd, i * 4 + m] for m in range(4)], axis=1) for i in range(4)]
         lhs = stacked(jnp.concatenate(rows, axis=0))
-        part = folded(jnp.dot(lhs, a[...], preferred_element_type=F32))
-        for i in range(4):
-            ms[rnd, i] = part[:, i * 128 : i * 128 + 128]
-        for z2 in z_peers:
-            send(ms.at[rnd, z2], mrs.at[rnd, z], rnd, MR, dev(z2, x, h, y, c))
-        mrs[rnd, z] = ms[rnd, z]
-        landed(mrs.at[rnd, pl.ds(0, 3)], rnd, MR)
-        mraw[rnd, c, mine_hz] = (mrs[rnd, 0] + mrs[rnd, 1]) + (mrs[rnd, 2] + mrs[rnd, 3])
-        for z2, h2 in zh_peers:
-            piece = mraw.at[rnd, c, mine_hz]
-            send(piece, piece, rnd, MG, dev(z2, x, h2, y, c))
-        landed(mraw.at[rnd, c, pl.ds(0, 7)], rnd, MG)
+        for n in range(2):
+            span = pl.ds(n * 256, 256)
+            part = folded(jnp.dot(lhs, a[:, n * 256 : n * 256 + 256], preferred_element_type=F32))
+            for i in range(8):
+                ms[rnd, i, :, n * 256 : n * 256 + 256] = part[i * 8 : i * 8 + 8]
+            for z2, h2 in zh_peers:
+                send(
+                    ms.at[rnd, h2 * 4 + z2, :, span], mrs.at[rnd, mine_hz, :, span], rnd, MR[n], dev(z2, x, h2, y, c)
+                )
+        mrs[rnd, mine_hz] = ms[rnd, mine_hz]
+        factor_blocks(15, 16)
+        linv[...] = work[:, RANK:]
+        for n in range(2):
+            span = pl.ds(n * 256, 256)
+            landed(mrs.at[rnd, pl.ds(0, 7), :, span], rnd, MR[n])
+            got = [mrs[rnd, i, :, n * 256 : n * 256 + 256] for i in range(8)]
+            mraw[rnd, c, mine_hz, :, n * 256 : n * 256 + 256] = ((got[0] + got[1]) + (got[2] + got[3])) + (
+                (got[4] + got[5]) + (got[6] + got[7])
+            )
+            for z2, h2 in zh_peers:
+                piece = mraw.at[rnd, c, mine_hz, :, span]
+                send(piece, piece, rnd, MG[n], dev(z2, x, h2, y, c))
+        for n in range(2):
+            landed(mraw.at[rnd, c, pl.ds(0, 7), :, pl.ds(n * 256, 256)], rnd, MG[n])
         send(mraw.at[rnd, c], mraw.at[rnd, c], rnd, MC, partner)
-        landed(mraw.at[rnd, o], rnd, MC)
-        for cc in range(2):
-            for hh in range(2):
-                for zz in range(4):
-                    for i in range(4):
-                        r0 = i * 32 + cc * 16 + hh * 8
-                        mfull[r0 : r0 + 8, zz * 128 : zz * 128 + 128] = mraw[
-                            rnd, cc, hh * 4 + zz, i * 8 : i * 8 + 8, :
-                        ]
-        mt[rnd] = jnp.dot(linv[rnd], mfull[...], precision=HIGHEST, preferred_element_type=F32)
-
-        rows = [mt[rnd, pl.ds(pl.multiple_of(i * 32 + c * 16 + h * 8, 8), 8), :] for i in range(4)]
-        lhs = stacked(jnp.concatenate(rows, axis=0))
-        part = folded(lax.dot_general(lhs, a[...], NT, preferred_element_type=F32))
+
+        def all_columns():
+            landed(mraw.at[rnd, o], rnd, MC)
+            for cc in range(2):
+                for i in range(8):
+                    r0 = (i // 2) * 32 + cc * 16 + (i % 2) * 8
+                    mfull[r0 : r0 + 8, :] = mraw[rnd, cc, i]
+
+        @pl.when(rnd == 0)
+        def _():
+            for i in range(8):
+                xl[i * 8 : i * 8 + 8, :] = mraw[rnd, c, i]
+
+        @pl.when(rnd > 0)
+        def _():
+            all_columns()
+            mt[rnd] = jnp.dot(linv[...], mfull[...], precision=HIGHEST, preferred_element_type=F32)
+            for i in range(4):
+                xl[i * 16 : i * 16 + 16, :] = mt[rnd, pl.ds(pl.multiple_of(i * 32 + c * 16, 16), 16), :]
+
+        part = folded(lax.dot_general(stacked(xl[...]), a[...], NT, preferred_element_type=F32))
         for i in range(4):
             for m in range(4):
-                xs[rnd, i * 4 + m] = part[i * 8 : i * 8 + 8, m * 256 : m * 256 + 256]
+                xs[rnd, i * 4 + m] = part[i * 16 : i * 16 + 16, m * 256 : m * 256 + 256]
         for x2, y2 in xy_peers:
             send(xs.at[rnd, x2 * 4 + y2], xrs.at[rnd, mine_xy], rnd, XR, dev(z, x2, h, y2, c))
         xrs[rnd, mine_xy] = xs[rnd, mine_xy]
+
+        @pl.when(rnd == 0)
+        def _():
+            all_columns()
+            mt[rnd] = mfull[...]
+
         gown[rnd] = lax.dot_general(
-            mt[rnd, pl.ds(pl.multiple_of(z * 32, 32), 32), :], mt[rnd], NT, precision=HIGHEST, preferred_element_type=F32
+            mt[rnd, pl.ds(pl.multiple_of((c * 4 + z) * 16, 16), 16), :],
+            mt[rnd], NT, precision=HIGHEST, preferred_element_type=F32,
         )
         for y2 in y_peers:
             send(gown.at[rnd], gys.at[rnd, y], rnd, GY, dev(z, x, h, y2, c))
@@ -245,17 +265,17 @@
         total = xrs[rnd, 0]
         for i in range(1, 16):
             total = total + xrs[rnd, i]
-        xt[rnd, c, mine_hy] = total
-        for h2, y2 in hy_peers:
-            piece = xt.at[rnd, c, mine_hy]
-            send(piece, piece, rnd, XG, dev(z, x, h2, y2, c))
+        xt[rnd, c, y] = total
+        for y2 in y_peers:
+            piece = xt.at[rnd, c, y]
+            send(piece, piece, rnd, XG, dev(z, x, h, y2, c))
         landed(gys.at[rnd, pl.ds(0, 3)], rnd, GY)
         gsum[rnd] = (gys[rnd, 0] + gys[rnd, 1]) + (gys[rnd, 2] + gys[rnd, 3])
         for x2 in x_peers:
             send(gsum.at[rnd], gxs.at[rnd, x], rnd, GX, dev(z, x2, h, y, c))
         gxs[rnd, x] = gsum[rnd]
 
-        landed(xt.at[rnd, c, pl.ds(0, 7)], rnd, XG)
+        landed(xt.at[rnd, c, pl.ds(0, 3)], rnd, XG)
         send(xt.at[rnd, c], xt.at[rnd, c], rnd, XC, partner)
 
         @pl.when(rnd == ROUNDS - 1)
@@ -270,7 +290,7 @@
 
         landed(xt.at[rnd, o], rnd, XC)
 
-        rows = [jnp.concatenate([xt[rnd, i // 2, (i % 2) * 4 + m] for m in range(4)], axis=1) for i in range(4)]
+        rows = [jnp.concatenate([xt[rnd, i, m] for m in range(4)], axis=1) for i in range(2)]
         lhs = stacked(jnp.concatenate(rows, axis=0))
         for n, (lo, size) in enumerate(PARTS):
             part = folded(jnp.dot(lhs, b[:, lo : lo + size], preferred_element_type=F32))
@@ -280,9 +300,9 @@
                 send(ps.at[rnd, z2, :, span], prs.at[rnd, z, :, span], rnd, PR[n], dev(z2, x, h, y, c))
         prs[rnd, z] = ps[rnd, z]
         landed(gxs.at[rnd, pl.ds(0, 3)], rnd, GX)
-        gfull[rnd, z] = (gxs[rnd, 0] + gxs[rnd, 1]) + (gxs[rnd, 2] + gxs[rnd, 3])
+        gfull[rnd, c, z] = (gxs[rnd, 0] + gxs[rnd, 1]) + (gxs[rnd, 2] + gxs[rnd, 3])
         for z2 in z_peers:
-            piece = gfull.at[rnd, z]
+            piece = gfull.at[rnd, c, z]
             send(piece, piece, rnd, GZ, dev(z2, x, h, y, c))
         for n, (lo, size) in enumerate(PARTS):
             span = pl.ds(lo, size)
@@ -291,15 +311,17 @@
             pt[rnd + 1, z, :, lo : lo + size] = (got[0] + got[1]) + (got[2] + got[3])
             for z2 in z_peers:
                 piece = pt.at[rnd + 1, z, :, span]
-                send(piece, piece, rnd, PG[n], dev(z2, x, h, y, c))
-        landed(gfull.at[rnd, pl.ds(0, 3)], rnd, GZ)
+                send(piece, piece, rnd, PG[n] + z, dev(z2, x, h, y, c))
+        landed(gfull.at[rnd, c, pl.ds(0, 3)], rnd, GZ)
+        send(gfull.at[rnd, c], gfull.at[rnd, c], rnd, GC, partner)
+        landed(gfull.at[rnd, o], rnd, GC)
         factor_start(rnd)
         factor_blocks(0, 6)
 
         @pl.when(rnd < ROUNDS - 1)
         def _():
-            for n, (lo, size) in enumerate(PARTS):
-                landed(pt.at[rnd + 1, pl.ds(0, 3), :, pl.ds(lo, size)], rnd, PG[n])
+            for z2 in z_peers:
+                gathered_p(rnd, z2)
             tokens_part(rnd + 1)
 
         return carry
@@ -309,9 +331,9 @@
     last = ROUNDS - 1
     for x2 in x_peers:
         send(pt.at[ROUNDS, z], cf.at[x, z], 2, PHASES, dev(z, x2, h, y, c))
-    for n, (lo, size) in enumerate(PARTS):
-        landed(pt.at[ROUNDS, pl.ds(0, 3), :, pl.ds(lo, size)], last, PG[n])
-    for z2 in z_peers:
+    for k in (1, 3, 2):
+        z2 = (z + k) % 4
+        gathered_p(last, z2)
         for x2 in x_peers:
             send(pt.at[ROUNDS, z2], cf.at[x, z2], 2, PHASES, dev(z, x2, h, y, c))
     landed(mg.at[pl.ds(0, 3), 0], 0, PHASES)
@@ -336,21 +358,24 @@
 
     def drain(rnd, carry):
         left(ycore.at[rnd], rnd, YC)
-        left(yrs.at[rnd, pl.ds(0, 7)], rnd, YR)
+        left(yrs.at[rnd, pl.ds(0, 3)], rnd, YR)
         left(yt.at[rnd, pl.ds(0, 15)], rnd, YG)
-        left(mrs.at[rnd, pl.ds(0, 3)], rnd, MR)
-        left(mraw.at[rnd, 0, pl.ds(0, 7)], rnd, MG)
+        for n in range(2):
+            span = pl.ds(n * 256, 256)
+            left(mrs.at[rnd, pl.ds(0, 7), :, span], rnd, MR[n])
+            left(mraw.at[rnd, 0, pl.ds(0, 7), :, span], rnd, MG[n])
         left(mraw.at[rnd, 0], rnd, MC)
         left(xrs.at[rnd, pl.ds(0, 15)], rnd, XR)
-        left(xt.at[rnd, 0, pl.ds(0, 7)], rnd, XG)
+        left(xt.at[rnd, 0, pl.ds(0, 3)], rnd, XG)
         left(xt.at[rnd, 0], rnd, XC)
         for n, (lo, size) in enumerate(PARTS):
             span = pl.ds(lo, size)
             left(prs.at[rnd, pl.ds(0, 3), :, span], rnd, PR[n])
-            left(pt.at[rnd, pl.ds(0, 3), :, span], rnd, PG[n])
+            left(pt.at[rnd, pl.ds(0, 3), :, span], rnd, PG[n] + z)
         left(gys.at[rnd, pl.ds(0, 3)], rnd, GY)
         left(gxs.at[rnd, pl.ds(0, 3)], rnd, GX)
-        left(gfull.at[rnd, pl.ds(0, 3)], rnd, GZ)
+        left(gfull.at[rnd, 0, pl.ds(0, 3)], rnd, GZ)
+        left(gfull.at[rnd, 0], rnd, GC)
         return carry
 
     lax.fori_loop(0, ROUNDS, drain, 0)
@@ -379,28 +404,29 @@
             vm((HID, RANK), F32),
             vm((RANK, HID), F32),
             vm((n + 1, 4, 8, HID), F32),
-            vm((n, 2, 8, 8, 256), F32),
-            vm((n, 8, 8, 256), F32),
-            vm((n, 8, 8, 256), F32),
-            vm((n, 8, 8, 256), F32),
-            vm((n, 16, 8, 256), F32),
-            vm((n, 4, 32, 128), F32),
-            vm((n, 4, 32, 128), F32),
-            vm((n, 2, 8, 32, 128), F32),
+            vm((n, 2, 4, 16, 256), F32),
+            vm((n, 4, 16, 256), F32),
+            vm((n, 4, 16, 256), F32),
+            vm((n, 4, 16, 256), F32),
+            vm((n, 16, 16, 256), F32),
+            vm((n, 8, 8, FEAT), F32),
+            vm((n, 8, 8, FEAT), F32),
+            vm((n, 2, 8, 8, FEAT), F32),
             vm((RANK, FEAT), F32),
             vm((n, RANK, FEAT), F32),
-            vm((n, 16, 8, 256), F32),
-            vm((n, 16, 8, 256), F32),
-            vm((n, 2, 8, 8, 256), F32),
+            vm((64, FEAT), F32),
+            vm((n, 16, 16, 256), F32),
+            vm((n, 16, 16, 256), F32),
+            vm((n, 2, 4, 16, 256), F32),
             vm((n, 4, 8, HID), F32),
             vm((n, 4, 8, HID), F32),
-            vm((n, 32, RANK), F32),
-            vm((n, 4, 32, RANK), F32),
-            vm((n, 32, RANK), F32),
-            vm((n, 4, 32, RANK), F32),
-            vm((n, 4, 32, RANK), F32),
+            vm((n, 16, RANK), F32),
+            vm((n, 4, 16, RANK), F32),
+            vm((n, 16, RANK), F32),
+            vm((n, 4, 16, RANK), F32),
+            vm((n, 2, 4, 16, RANK), F32),
             vm((RANK, 2 * RANK), F32),
-            vm((n, RANK, RANK), F32),
+            vm((RANK, RANK), F32),
             vm((4, 4, 8, HID), F32),
             vm((4, 2, RANK, 256), F32),
             pltpu.SemaphoreType.DMA((3,)),
@@ -408,7 +434,7 @@
             pltpu.SemaphoreType.DMA((n, PHASES + 1)),
         ],
         compiler_params=pltpu.CompilerParams(
-            collective_id=0, has_side_effects=True, vmem_limit_bytes=48 * 2**20
+            collective_id=0, has_side_effects=True, vmem_limit_bytes=60 * 2**20
         ),
     )(activations, grad_out, sketch)
 

time: 173 us -> 170 us (0.983)
  Pallas kernels: 168 us -> 164 us
    pallas_call x1, Pallas kernels: 168 us -> 164 us  [body(): pl.pallas_call(kernel, name='range_finder', out_shape=(jax.ShapeDtypeStru...]
    unnamed x6 -> x2, local copies, waits for them, and re-layouts: 4.99 us -> 4.37 us
where the time goes in v4:
time: 170 us; the launch traced here: 169 us
  Pallas kernels  164 us (96%)
  local copies, waits for them, and re-layouts  4.37 us (3%)
    pallas_call x1, Pallas kernels, body(): pl.pallas_call(kernel, name='range_finder', out_shape=(jax.ShapeDtypeStru...  164 us
    unnamed x2, local copies, waits for them, and re-layouts  4.37 us

profile of v4, /device:TPU:1, one launch (start us, length us, event | category | flops | bytes accessed | tf_op | source)
XLA Modules:
  0.0 169.4 jit_solution(7641106716550855159)
XLA Ops:
  0.6 164.4 %range_finder.1 = (f32[2048,128]{1,0:T(8,128)}, f32[128,1664]{1,0:T(8,128)}) custom-call(bf16[1024,2048]{1,0:T(8,128)(2,1)} %a_hbm.1, bf16[1024,1664]{1,0:T(8,128)(2,1)} %b_hbm.1, f32[1664,128]{1,0:T(8,128)} %s_hbm.1), custom_call_target="tpu_custom_call" | custom-call | tf_op jit(solution)/shard_map/range_finder/pallas_call | solution.py:392
  165.0 2.3 %copy.7 = f32[2048,128]{1,0:T(8,128)} copy(f32[2048,128]{1,0:T(8,128)} %get-tuple-element.4) | data formatting | bytes 2097152
  167.3 2.1 %copy.8 = f32[128,1664]{1,0:T(8,128)} copy(f32[128,1664]{1,0:T(8,128)} %get-tuple-element.5) | data formatting | bytes 1703936

commit v5 on v4

--- a/solution.py
+++ b/solution.py
@@ -21,10 +21,10 @@
 NT = (((1,), (1,)), ((), ()))
 TN = (((0,), (0,)), ((), ()))
 PARTS = ((0, 896), (896, 768))
-YC, YR, YG, MRA, MRB, MGA, MGB, MC, XR, XG, XC, PRA, PRB, GY, GX, GZ, GC = range(17)
+YR, YG, MRA, MRB, MGA, MGB, MC, XR, XG, PRA, PRB, GY, GX, GZ, GC = range(15)
 MR, MG, PR = (MRA, MRB), (MGA, MGB), (PRA, PRB)
-PG = (17, 21)
-PHASES = 25
+PG = (15, 19)
+PHASES = 23
 XY = (
     (2, 2), (2, 1), (2, 3), (1, 2), (3, 2), (1, 1), (1, 3), (3, 1), (3, 3),
     (2, 0), (0, 2), (1, 0), (3, 0), (0, 1), (0, 3),
@@ -47,8 +47,8 @@
 
 def kernel(
     a_hbm, b_hbm, s_hbm, basis_ref, coef_ref,
-    a, b, s, st, pt, ysend, ycore, yown, yrs, yt, ms, mrs, mraw, mfull, mt, xl, xs, xrs, xt,
-    ps, prs, gown, gys, gsum, gxs, gfull, work, linv, cf, mg,
+    a, b, s, st, pt, ysend, yrs, yt, ms, mrs, mraw, mfull, mt, xl, xs, xrs, xt,
+    ps, prs, gown, gys, gsum, gxs, gfull, work, cf, mg,
     load_sem, send_sem, recv_sem,
 ):
     z, x, j = lax.axis_index("dp"), lax.axis_index("row"), lax.axis_index("col")
@@ -58,6 +58,7 @@
     o = 1 - c
     mine_xy = x * 4 + y
     mine_hz = h * 4 + z
+    mine_cy = c * 4 + y
 
     def dev(z_, x_, h_, y_, c_):
         return (z_, x_, (h_ * 4 + y_) * 2 + c_)
@@ -67,6 +68,7 @@
     zh_peers = [((z + dz) % 4, (h + dh) % 2) for dz, dh in ZH]
     z_peers = [(z + k) % 4 for k in (2, 1, 3)]
     y_peers = [(y + k) % 4 for k in (2, 1, 3)]
+    yc_peers = [((y + k) % 4, c2) for k in (2, 1, 3) for c2 in (c, o)] + [(y, o)]
     x_peers = [(x + k) % 4 for k in (2, 1, 3)]
 
     barrier = pltpu.get_barrier_semaphore()
@@ -84,11 +86,13 @@
     for load in loads:
         load.start()
 
-    for x2, y2 in xy_peers:
-        greet(dev(z, x2, h, y2, c))
+    for (x2, y2), (dx, _) in zip(xy_peers, XY):
+        if dx:
+            greet(dev(z, x2, h, y2, c))
     for z2, h2 in zh_peers:
         greet(dev(z2, x, h2, y, c))
-    greet(partner)
+    for y2, c2 in yc_peers:
+        greet(dev(z, x, h, y2, c2))
 
     def send(src, dst, rnd, phase, device):
         pltpu.make_async_remote_copy(
@@ -156,42 +160,52 @@
     def factor_blocks(lo, hi):
         lax.fori_loop(lo, hi, factor_block, 0)
 
-    def tokens_part(rnd):
-        lhs = stacked(pt[rnd].reshape(32, HID))
-        part = folded(lax.dot_general(lhs, b[...], NT, preferred_element_type=F32))
+    def tokens_part(rnd, ready):
+        part = None
+        for n, (lo, size) in enumerate(PARTS):
+            ready(n)
+            lhs = stacked(pt[rnd, :, :, lo : lo + size].reshape(32, size))
+            term = folded(lax.dot_general(lhs, b[:, lo : lo + size], NT, preferred_element_type=F32))
+            part = term if part is None else part + term
         for i in range(2):
             for m in range(4):
-                ysend[rnd, i, m] = part[i * 16 : i * 16 + 16, m * 256 : m * 256 + 256]
+                ysend[rnd, i * 4 + m] = part[i * 16 : i * 16 + 16, m * 256 : m * 256 + 256]
 
     loads[0].wait()
     st[...] = s[...].T
     pt[0] = st[pl.ds(pl.multiple_of(x * 32, 32), 32), :].reshape(4, 8, HID)
-    work[:, :RANK] = eye
-    work[:, RANK:] = eye
     loads[1].wait()
-    tokens_part(0)
+    tokens_part(0, lambda n: None)
     loads[2].wait()
 
-    pl.semaphore_wait(barrier, 23)
-
-    def gathered_p(rnd, z2):
-        for n, (lo, size) in enumerate(PARTS):
-            landed(pt.at[rnd + 1, z2, :, pl.ds(lo, size)], rnd, PG[n] + z2)
+    pl.semaphore_wait(barrier, 26)
+
+    def gathered_p(rnd, n, z2):
+        lo, size = PARTS[n]
+        landed(pt.at[rnd + 1, z2, :, pl.ds(lo, size)], rnd, PG[n] + z2)
 
     def one_round(rnd, carry):
-        send(ysend.at[rnd, o], ycore.at[rnd], rnd, YC, partner)
-        landed(ycore.at[rnd], rnd, YC)
-        yown[rnd] = ysend[rnd, c] + ycore[rnd]
-        for y2 in y_peers:
-            send(yown.at[rnd, y2], yrs.at[rnd, y], rnd, YR, dev(z, x, h, y2, c))
-        yrs[rnd, y] = yown[rnd, y]
-        factor_blocks(6, 9)
-        landed(yrs.at[rnd, pl.ds(0, 3)], rnd, YR)
-        yt[rnd, mine_xy] = (yrs[rnd, 0] + yrs[rnd, 1]) + (yrs[rnd, 2] + yrs[rnd, 3])
+        for y2, c2 in yc_peers:
+            send(ysend.at[rnd, c2 * 4 + y2], yrs.at[rnd, mine_cy], rnd, YR, dev(z, x, h, y2, c2))
+        yrs[rnd, mine_cy] = ysend[rnd, mine_cy]
+
+        @pl.when(rnd > 0)
+        def _():
+            landed(gfull.at[rnd - 1, o], rnd - 1, GC)
+            factor_start(rnd - 1)
+            factor_blocks(0, 4)
+
+        landed(yrs.at[rnd, pl.ds(0, 7)], rnd, YR)
+        got = [yrs[rnd, i] for i in range(8)]
+        yt[rnd, mine_xy] = ((got[0] + got[1]) + (got[2] + got[3])) + ((got[4] + got[5]) + (got[6] + got[7]))
         for x2, y2 in xy_peers:
             piece = yt.at[rnd, mine_xy]
             send(piece, piece, rnd, YG, dev(z, x2, h, y2, c))
-        factor_blocks(9, 15)
+
+        @pl.when(rnd > 0)
+        def _():
+            factor_blocks(4, 9)
+
         landed(yt.at[rnd, pl.ds(0, 15)], rnd, YG)
 
         rows = [jnp.concatenate([yt[rnd, i * 4 + m] for m in range(4)], axis=1) for i in range(4)]
@@ -206,8 +220,11 @@
                     ms.at[rnd, h2 * 4 + z2, :, span], mrs.at[rnd, mine_hz, :, span], rnd, MR[n], dev(z2, x, h2, y, c)
                 )
         mrs[rnd, mine_hz] = ms[rnd, mine_hz]
-        factor_blocks(15, 16)
-        linv[...] = work[:, RANK:]
+
+        @pl.when(rnd > 0)
+        def _():
+            factor_blocks(9, 14)
+
         for n in range(2):
             span = pl.ds(n * 256, 256)
             landed(mrs.at[rnd, pl.ds(0, 7), :, span], rnd, MR[n])
@@ -218,6 +235,11 @@
             for z2, h2 in zh_peers:
                 piece = mraw.at[rnd, c, mine_hz, :, span]
                 send(piece, piece, rnd, MG[n], dev(z2, x, h2, y, c))
+
+        @pl.when(rnd > 0)
+        def _():
+            factor_blocks(14, 16)
+
         for n in range(2):
             landed(mraw.at[rnd, c, pl.ds(0, 7), :, pl.ds(n * 256, 256)], rnd, MG[n])
         send(mraw.at[rnd, c], mraw.at[rnd, c], rnd, MC, partner)
@@ -237,7 +259,7 @@
         @pl.when(rnd > 0)
         def _():
             all_columns()
-            mt[rnd] = jnp.dot(linv[...], mfull[...], precision=HIGHEST, preferred_element_type=F32)
+            mt[rnd] = jnp.dot(work[:, RANK:], mfull[...], precision=HIGHEST, preferred_element_type=F32)
             for i in range(4):
                 xl[i * 16 : i * 16 + 16, :] = mt[rnd, pl.ds(pl.multiple_of(i * 32 + c * 16, 16), 16), :]
 
@@ -265,32 +287,19 @@
         total = xrs[rnd, 0]
         for i in range(1, 16):
             total = total + xrs[rnd, i]
-        xt[rnd, c, y] = total
-        for y2 in y_peers:
-            piece = xt.at[rnd, c, y]
-            send(piece, piece, rnd, XG, dev(z, x, h, y2, c))
+        xt[rnd, mine_cy] = total
+        for y2, c2 in yc_peers:
+            piece = xt.at[rnd, mine_cy]
+            send(piece, piece, rnd, XG, dev(z, x, h, y2, c2))
         landed(gys.at[rnd, pl.ds(0, 3)], rnd, GY)
         gsum[rnd] = (gys[rnd, 0] + gys[rnd, 1]) + (gys[rnd, 2] + gys[rnd, 3])
         for x2 in x_peers:
             send(gsum.at[rnd], gxs.at[rnd, x], rnd, GX, dev(z, x2, h, y, c))
         gxs[rnd, x] = gsum[rnd]
 
-        landed(xt.at[rnd, c, pl.ds(0, 3)], rnd, XG)
-        send(xt.at[rnd, c], xt.at[rnd, c], rnd, XC, partner)
-
-        @pl.when(rnd == ROUNDS - 1)
-        def _():
-            for y2 in y_peers:
-                send(
-                    mt.at[rnd, :, pl.ds(pl.multiple_of(c * 256, 256), 256)],
-                    mg.at[y, c],
-                    0, PHASES,
-                    dev(z, x, h, y2, c),
-                )
-
-        landed(xt.at[rnd, o], rnd, XC)
-
-        rows = [jnp.concatenate([xt[rnd, i, m] for m in range(4)], axis=1) for i in range(2)]
+        landed(xt.at[rnd, pl.ds(0, 7)], rnd, XG)
+
+        rows = [jnp.concatenate([xt[rnd, i * 4 + m] for m in range(4)], axis=1) for i in range(2)]
         lhs = stacked(jnp.concatenate(rows, axis=0))
         for n, (lo, size) in enumerate(PARTS):
             part = folded(jnp.dot(lhs, b[:, lo : lo + size], preferred_element_type=F32))
@@ -299,6 +308,17 @@
                 span = pl.ds(lo, size)
                 send(ps.at[rnd, z2, :, span], prs.at[rnd, z, :, span], rnd, PR[n], dev(z2, x, h, y, c))
         prs[rnd, z] = ps[rnd, z]
+
+        @pl.when(rnd == ROUNDS - 1)
+        def _():
+            for y2 in y_peers:
+                send(
+                    mt.at[rnd, :, pl.ds(pl.multiple_of(c * 256, 256), 256)],
+                    mg.at[y, c],
+                    0, PHASES,
+                    dev(z, x, h, y2, c),
+                )
+
         landed(gxs.at[rnd, pl.ds(0, 3)], rnd, GX)
         gfull[rnd, c, z] = (gxs[rnd, 0] + gxs[rnd, 1]) + (gxs[rnd, 2] + gxs[rnd, 3])
         for z2 in z_peers:
@@ -314,15 +334,14 @@
                 send(piece, piece, rnd, PG[n] + z, dev(z2, x, h, y, c))
         landed(gfull.at[rnd, c, pl.ds(0, 3)], rnd, GZ)
         send(gfull.at[rnd, c], gfull.at[rnd, c], rnd, GC, partner)
-        landed(gfull.at[rnd, o], rnd, GC)
-        factor_start(rnd)
-        factor_blocks(0, 6)
 
         @pl.when(rnd < ROUNDS - 1)
         def _():
-            for z2 in z_peers:
-                gathered_p(rnd, z2)
-            tokens_part(rnd + 1)
+            def ready(n):
+                for z2 in z_peers:
+                    gathered_p(rnd, n, z2)
+
+            tokens_part(rnd + 1, ready)
 
         return carry
 
@@ -331,9 +350,13 @@
     last = ROUNDS - 1
     for x2 in x_peers:
         send(pt.at[ROUNDS, z], cf.at[x, z], 2, PHASES, dev(z, x2, h, y, c))
+    landed(gfull.at[last, o], last, GC)
+    factor_start(last)
+    factor_blocks(0, 4)
     for k in (1, 3, 2):
         z2 = (z + k) % 4
-        gathered_p(last, z2)
+        for n in range(2):
+            gathered_p(last, n, z2)
         for x2 in x_peers:
             send(pt.at[ROUNDS, z2], cf.at[x, z2], 2, PHASES, dev(z, x2, h, y, c))
     landed(mg.at[pl.ds(0, 3), 0], 0, PHASES)
@@ -343,7 +366,7 @@
     for cc in range(2):
         mg[y, cc] = mt[last, :, cc * 256 : cc * 256 + 256]
     cf[x] = pt[ROUNDS]
-    factor_blocks(6, 16)
+    factor_blocks(4, 16)
     final = work[:, RANK:]
     scaled = final * math.sqrt(D)
     landed(mg.at[pl.ds(0, 3), 0], 1, PHASES)
@@ -357,8 +380,7 @@
     coef_ref[...] = jnp.dot(final, cf[...].reshape(RANK, HID), precision=HIGHEST, preferred_element_type=F32)
 
     def drain(rnd, carry):
-        left(ycore.at[rnd], rnd, YC)
-        left(yrs.at[rnd, pl.ds(0, 3)], rnd, YR)
+        left(yrs.at[rnd, pl.ds(0, 7)], rnd, YR)
         left(yt.at[rnd, pl.ds(0, 15)], rnd, YG)
         for n in range(2):
             span = pl.ds(n * 256, 256)
@@ -366,8 +388,7 @@
             left(mraw.at[rnd, 0, pl.ds(0, 7), :, span], rnd, MG[n])
         left(mraw.at[rnd, 0], rnd, MC)
         left(xrs.at[rnd, pl.ds(0, 15)], rnd, XR)
-        left(xt.at[rnd, 0, pl.ds(0, 3)], rnd, XG)
-        left(xt.at[rnd, 0], rnd, XC)
+        left(xt.at[rnd, pl.ds(0, 7)], rnd, XG)
         for n, (lo, size) in enumerate(PARTS):
             span = pl.ds(lo, size)
             left(prs.at[rnd, pl.ds(0, 3), :, span], rnd, PR[n])
@@ -404,10 +425,8 @@
             vm((HID, RANK), F32),
             vm((RANK, HID), F32),
             vm((n + 1, 4, 8, HID), F32),
-            vm((n, 2, 4, 16, 256), F32),
-            vm((n, 4, 16, 256), F32),
-            vm((n, 4, 16, 256), F32),
-            vm((n, 4, 16, 256), F32),
+            vm((n, 8, 16, 256), F32),
+            vm((n, 8, 16, 256), F32),
             vm((n, 16, 16, 256), F32),
             vm((n, 8, 8, FEAT), F32),
             vm((n, 8, 8, FEAT), F32),
@@ -417,7 +436,7 @@
             vm((64, FEAT), F32),
             vm((n, 16, 16, 256), F32),
             vm((n, 16, 16, 256), F32),
-            vm((n, 2, 4, 16, 256), F32),
+            vm((n, 8, 16, 256), F32),
             vm((n, 4, 8, HID), F32),
             vm((n, 4, 8, HID), F32),
             vm((n, 16, RANK), F32),
@@ -426,7 +445,6 @@
             vm((n, 4, 16, RANK), F32),
             vm((n, 2, 4, 16, RANK), F32),
             vm((RANK, 2 * RANK), F32),
-            vm((RANK, RANK), F32),
             vm((4, 4, 8, HID), F32),
             vm((4, 2, RANK, 256), F32),
             pltpu.SemaphoreType.DMA((3,)),
@@ -434,7 +452,7 @@
             pltpu.SemaphoreType.DMA((n, PHASES + 1)),
         ],
         compiler_params=pltpu.CompilerParams(
-            collective_id=0, has_side_effects=True, vmem_limit_bytes=60 * 2**20
+            collective_id=0, has_side_effects=True, vmem_limit_bytes=50 * 2**20
         ),
     )(activations, grad_out, sketch)
 

time: 170 us -> 158 us (0.929)
  Pallas kernels: 164 us -> 154 us
    pallas_call x1, Pallas kernels: 164 us -> 154 us  [body(): pl.pallas_call(kernel, name='range_finder', out_shape=(jax.ShapeDtypeStru...]
    unnamed x2 -> x4, local copies, waits for them, and re-layouts: 4.37 us -> 3.02 us
where the time goes in v5:
time: 158 us; the launch traced here: 157 us
  Pallas kernels  154 us (97%)
  local copies, waits for them, and re-layouts  3.02 us (2%)
    pallas_call x1, Pallas kernels, body(): pl.pallas_call(kernel, name='range_finder', out_shape=(jax.ShapeDtypeStru...  154 us

profile of v5, /device:TPU:1, one launch (start us, length us, event | category | flops | bytes accessed | tf_op | source)
XLA Modules:
  0.0 157.4 jit_solution(496569539457454583)
XLA Ops:
  0.6 0.0 copy-start
  0.6 1.1 copy-done
  1.8 153.7 %range_finder.1 = (f32[2048,128]{1,0:T(8,128)S(1)}, f32[128,1664]{1,0:T(8,128)S(1)}) custom-call(bf16[1024,2048]{1,0:T(8,128)(2,1)} %a_hbm.1, bf16[1024,1664]{1,0:T(8,128)(2,1)} %b_hbm.1, f32[1664,128]{1,0:T(8,128)S(1)} %copy-done), custom_call_target="tpu_custom_call" | custom-call | tf_op jit(solution)/shard_map/range_finder/pallas_call | solution.py:413
  155.5 1.0 copy.7
  156.5 0.9 copy.8
Async XLA Ops:
  0.6 1.2 copy-start

commit v6 on v5

--- a/solution.py
+++ b/solution.py
@@ -40,6 +40,21 @@
     return jnp.concatenate([high, mid, low], axis=0)
 
 
+def outer(left, right):
+    def three(mat):
+        high = mat.astype(BF16).astype(F32)
+        mid = (mat - high).astype(BF16).astype(F32)
+        return high, mid, (mat - high - mid).astype(BF16).astype(F32)
+
+    lh, lm, ll = three(left)
+    rh, rm, rl = three(right)
+    return lax.dot_general(
+        jnp.concatenate([lh, lh, lm, lh, ll, lm], axis=0).astype(BF16),
+        jnp.concatenate([rh, rm, rh, rl, rh, rm], axis=0).astype(BF16),
+        TN, preferred_element_type=F32,
+    )
+
+
 def folded(wide):
     rows = wide.shape[0] // 3
     return wide[:rows] + (wide[rows : 2 * rows] + wide[2 * rows :])
@@ -47,7 +62,7 @@
 
 def kernel(
     a_hbm, b_hbm, s_hbm, basis_ref, coef_ref,
-    a, b, s, st, pt, ysend, yrs, yt, ms, mrs, mraw, mfull, mt, xl, xs, xrs, xt,
+    a, b, s, st, pt, yacc, ysend, yrs, yt, ms, mrs, mraw, mfull, mt, xl, xs, xrs, xt,
     ps, prs, gown, gys, gsum, gxs, gfull, work, cf, mg,
     load_sem, send_sem, recv_sem,
 ):
@@ -152,41 +167,53 @@
             ue = ue + weight * spread(ep[m : m + 1])
         work[pl.ds(r0, 8), RANK:] = ue
         rest = jnp.where(lane >= r0 + 8, ug, 0.0)
-        work[...] -= lax.dot_general(
-            rest, jnp.concatenate([ug, ue], axis=1), TN, precision=HIGHEST, preferred_element_type=F32
-        )
+        work[...] -= outer(rest, jnp.concatenate([ug, ue], axis=1))
         return carry
 
     def factor_blocks(lo, hi):
         lax.fori_loop(lo, hi, factor_block, 0)
 
     def tokens_part(rnd, ready):
-        part = None
+        sides = []
         for n, (lo, size) in enumerate(PARTS):
             ready(n)
-            lhs = stacked(pt[rnd, :, :, lo : lo + size].reshape(32, size))
-            term = folded(lax.dot_general(lhs, b[:, lo : lo + size], NT, preferred_element_type=F32))
-            part = term if part is None else part + term
-        for i in range(2):
-            for m in range(4):
-                ysend[rnd, i * 4 + m] = part[i * 16 : i * 16 + 16, m * 256 : m * 256 + 256]
+            sides.append(stacked(pt[rnd, :, :, lo : lo + size].reshape(32, size)))
+            if n == 0:
+                part = folded(lax.dot_general(sides[0], b[:, lo : lo + size], NT, preferred_element_type=F32))
+                for m in range(4):
+                    yacc[m] = part[:, m * 256 : m * 256 + 256]
+        lo, size = PARTS[1]
+        for k in (2, 1, 3, 0):
+            y2 = (y + k) % 4
+            rows = b[pl.ds(pl.multiple_of(y2 * 256, 256), 256), lo : lo + size]
+            quarter = yacc[y2] + folded(lax.dot_general(sides[1], rows, NT, preferred_element_type=F32))
+            ysend[rnd, y2] = quarter[:16]
+            ysend[rnd, 4 + y2] = quarter[16:]
+            for c2 in (c, o) if k else (o,):
+                send(ysend.at[rnd, c2 * 4 + y2], yrs.at[rnd, mine_cy], rnd, YR, dev(z, x, h, y2, c2))
 
     loads[0].wait()
     st[...] = s[...].T
     pt[0] = st[pl.ds(pl.multiple_of(x * 32, 32), 32), :].reshape(4, 8, HID)
     loads[1].wait()
-    tokens_part(0, lambda n: None)
+
+    def begin(n):
+        if n == 1:
+            pl.semaphore_wait(barrier, 26)
+
+    tokens_part(0, begin)
     loads[2].wait()
 
-    pl.semaphore_wait(barrier, 26)
+    def to_row(z2, n):
+        span = pl.ds(*PARTS[n])
+        for x2 in x_peers:
+            send(pt.at[ROUNDS, z2, :, span], cf.at[x, z2, :, span], 2, PHASES, dev(z, x2, h, y, c))
 
     def gathered_p(rnd, n, z2):
         lo, size = PARTS[n]
         landed(pt.at[rnd + 1, z2, :, pl.ds(lo, size)], rnd, PG[n] + z2)
 
     def one_round(rnd, carry):
-        for y2, c2 in yc_peers:
-            send(ysend.at[rnd, c2 * 4 + y2], yrs.at[rnd, mine_cy], rnd, YR, dev(z, x, h, y2, c2))
         yrs[rnd, mine_cy] = ysend[rnd, mine_cy]
 
         @pl.when(rnd > 0)
@@ -263,12 +290,15 @@
             for i in range(4):
                 xl[i * 16 : i * 16 + 16, :] = mt[rnd, pl.ds(pl.multiple_of(i * 32 + c * 16, 16), 16), :]
 
-        part = folded(lax.dot_general(stacked(xl[...]), a[...], NT, preferred_element_type=F32))
-        for i in range(4):
-            for m in range(4):
-                xs[rnd, i * 4 + m] = part[i * 16 : i * 16 + 16, m * 256 : m * 256 + 256]
-        for x2, y2 in xy_peers:
-            send(xs.at[rnd, x2 * 4 + y2], xrs.at[rnd, mine_xy], rnd, XR, dev(z, x2, h, y2, c))
+        lhs = stacked(xl[...])
+        for k in (2, 1, 3, 0):
+            y2 = (y + k) % 4
+            rows = a[pl.ds(pl.multiple_of(y2 * 256, 256), 256), :]
+            part = folded(lax.dot_general(lhs, rows, NT, preferred_element_type=F32))
+            for i in range(4):
+                xs[rnd, i * 4 + y2] = part[i * 16 : i * 16 + 16]
+            for x2 in x_peers + ([x] if k else []):
+                send(xs.at[rnd, x2 * 4 + y2], xrs.at[rnd, mine_xy], rnd, XR, dev(z, x2, h, y2, c))
         xrs[rnd, mine_xy] = xs[rnd, mine_xy]
 
         @pl.when(rnd == 0)
@@ -307,6 +337,12 @@
             for z2 in z_peers:
                 span = pl.ds(lo, size)
                 send(ps.at[rnd, z2, :, span], prs.at[rnd, z, :, span], rnd, PR[n], dev(z2, x, h, y, c))
+            if n == 0:
+                landed(gxs.at[rnd, pl.ds(0, 3)], rnd, GX)
+                gfull[rnd, c, z] = (gxs[rnd, 0] + gxs[rnd, 1]) + (gxs[rnd, 2] + gxs[rnd, 3])
+                for z2 in z_peers:
+                    piece = gfull.at[rnd, c, z]
+                    send(piece, piece, rnd, GZ, dev(z2, x, h, y, c))
         prs[rnd, z] = ps[rnd, z]
 
         @pl.when(rnd == ROUNDS - 1)
@@ -319,11 +355,6 @@
                     dev(z, x, h, y2, c),
                 )
 
-        landed(gxs.at[rnd, pl.ds(0, 3)], rnd, GX)
-        gfull[rnd, c, z] = (gxs[rnd, 0] + gxs[rnd, 1]) + (gxs[rnd, 2] + gxs[rnd, 3])
-        for z2 in z_peers:
-            piece = gfull.at[rnd, c, z]
-            send(piece, piece, rnd, GZ, dev(z2, x, h, y, c))
         for n, (lo, size) in enumerate(PARTS):
             span = pl.ds(lo, size)
             landed(prs.at[rnd, pl.ds(0, 3), :, span], rnd, PR[n])
@@ -332,6 +363,11 @@
             for z2 in z_peers:
                 piece = pt.at[rnd + 1, z, :, span]
                 send(piece, piece, rnd, PG[n] + z, dev(z2, x, h, y, c))
+
+            @pl.when(rnd == ROUNDS - 1)
+            def _():
+                to_row(z, n)
+
         landed(gfull.at[rnd, c, pl.ds(0, 3)], rnd, GZ)
         send(gfull.at[rnd, c], gfull.at[rnd, c], rnd, GC, partner)
 
@@ -348,17 +384,15 @@
     lax.fori_loop(0, ROUNDS, one_round, 0)
 
     last = ROUNDS - 1
-    for x2 in x_peers:
-        send(pt.at[ROUNDS, z], cf.at[x, z], 2, PHASES, dev(z, x2, h, y, c))
     landed(gfull.at[last, o], last, GC)
     factor_start(last)
-    factor_blocks(0, 4)
-    for k in (1, 3, 2):
-        z2 = (z + k) % 4
-        for n in range(2):
+    factor_blocks(0, 2)
+    for n in range(2):
+        for k in (1, 3, 2):
+            z2 = (z + k) % 4
             gathered_p(last, n, z2)
-        for x2 in x_peers:
-            send(pt.at[ROUNDS, z2], cf.at[x, z2], 2, PHASES, dev(z, x2, h, y, c))
+            to_row(z2, n)
+        factor_blocks(2 + n * 2, 4 + n * 2)
     landed(mg.at[pl.ds(0, 3), 0], 0, PHASES)
     for y2 in y_peers:
         piece = mg.at[y2, c]
@@ -366,7 +400,7 @@
     for cc in range(2):
         mg[y, cc] = mt[last, :, cc * 256 : cc * 256 + 256]
     cf[x] = pt[ROUNDS]
-    factor_blocks(4, 16)
+    factor_blocks(6, 16)
     final = work[:, RANK:]
     scaled = final * math.sqrt(D)
     landed(mg.at[pl.ds(0, 3), 0], 1, PHASES)
@@ -425,6 +459,7 @@
             vm((HID, RANK), F32),
             vm((RANK, HID), F32),
             vm((n + 1, 4, 8, HID), F32),
+            vm((4, 32, 256), F32),
             vm((n, 8, 16, 256), F32),
             vm((n, 8, 16, 256), F32),
             vm((n, 16, 16, 256), F32),

time: 158 us -> 157 us (level)
  no operation moved by 1% of the time
where the time goes in v6:
time: 157 us
  Pallas kernels  153 us (97%)
  local copies, waits for them, and re-layouts  3.02 us (2%)
    pallas_call x1, Pallas kernels, body(): pl.pallas_call(kernel, name='range_finder', out_shape=(jax.ShapeDtypeStru...  153 us

profile of v6, /device:TPU:1, one launch (start us, length us, event | category | flops | bytes accessed | tf_op | source)
XLA Modules:
  0.0 156.5 jit_solution(16341809280202223321)
XLA Ops:
  0.6 0.0 copy-start
  0.6 1.1 copy-done
  1.8 152.9 %range_finder.1 = (f32[2048,128]{1,0:T(8,128)S(1)}, f32[128,1664]{1,0:T(8,128)S(1)}) custom-call(bf16[1024,2048]{1,0:T(8,128)(2,1)} %a_hbm.1, bf16[1024,1664]{1,0:T(8,128)(2,1)} %b_hbm.1, f32[1664,128]{1,0:T(8,128)S(1)} %copy-done), custom_call_target="tpu_custom_call" | custom-call | tf_op jit(solution)/shard_map/range_finder/pallas_call | solution.py:447
  154.7 1.0 copy.7
  155.6 0.9 copy.8
Async XLA Ops:
  0.6 1.2 copy-start

commit v7 on v6

--- a/solution.py
+++ b/solution.py
@@ -20,11 +20,12 @@
 FEAT = 512
 NT = (((1,), (1,)), ((), ()))
 TN = (((0,), (0,)), ((), ()))
-PARTS = ((0, 896), (896, 768))
-YR, YG, MRA, MRB, MGA, MGB, MC, XR, XG, PRA, PRB, GY, GX, GZ, GC = range(15)
-MR, MG, PR = (MRA, MRB), (MGA, MGB), (PRA, PRB)
-PG = (15, 19)
-PHASES = 23
+PARTS = ((0, 640), (640, 512), (1152, 512))
+HALVES = ((0, 256), (256, 256))
+YR, YG, MC, XR, XG, GY, GX, GZ, GC = range(9)
+MR, MG, PR = range(9, 12), range(12, 15), range(15, 18)
+PG = range(18, 30, 4)
+PHASES = 30
 XY = (
     (2, 2), (2, 1), (2, 3), (1, 2), (3, 2), (1, 1), (1, 3), (3, 1), (3, 3),
     (2, 0), (0, 2), (1, 0), (3, 0), (0, 1), (0, 3),
@@ -93,11 +94,15 @@
 
     loads = [
         pltpu.make_async_copy(s_hbm, s, load_sem.at[0]),
-        pltpu.make_async_copy(b_hbm, b, load_sem.at[1]),
+    ]
+    for n, (lo, size) in enumerate(PARTS):
+        span = pl.ds(lo, size)
+        loads.append(pltpu.make_async_copy(b_hbm.at[:, span], b.at[:, span], load_sem.at[1 + n]))
+    loads.append(
         pltpu.make_async_copy(
-            a_hbm.at[:, pl.ds(pl.multiple_of(y * FEAT, FEAT), FEAT)], a, load_sem.at[2]
-        ),
-    ]
+            a_hbm.at[:, pl.ds(pl.multiple_of(y * FEAT, FEAT), FEAT)], a, load_sem.at[1 + len(PARTS)]
+        )
+    )
     for load in loads:
         load.start()
 
@@ -174,19 +179,20 @@
         lax.fori_loop(lo, hi, factor_block, 0)
 
     def tokens_part(rnd, ready):
-        sides = []
         for n, (lo, size) in enumerate(PARTS):
             ready(n)
-            sides.append(stacked(pt[rnd, :, :, lo : lo + size].reshape(32, size)))
-            if n == 0:
-                part = folded(lax.dot_general(sides[0], b[:, lo : lo + size], NT, preferred_element_type=F32))
+            lhs = stacked(pt[rnd, :, :, lo : lo + size].reshape(32, size))
+            if n < len(PARTS) - 1:
+                part = folded(lax.dot_general(lhs, b[:, lo : lo + size], NT, preferred_element_type=F32))
                 for m in range(4):
-                    yacc[m] = part[:, m * 256 : m * 256 + 256]
-        lo, size = PARTS[1]
+                    quarter = part[:, m * 256 : m * 256 + 256]
+                    yacc[m] = yacc[m] + quarter if n else quarter
         for k in (2, 1, 3, 0):
             y2 = (y + k) % 4
             rows = b[pl.ds(pl.multiple_of(y2 * 256, 256), 256), lo : lo + size]
-            quarter = yacc[y2] + folded(lax.dot_general(sides[1], rows, NT, preferred_element_type=F32))
+            quarter = folded(lax.dot_general(lhs, rows, NT, preferred_element_type=F32))
+            if len(PARTS) > 1:
+                quarter = yacc[y2] + quarter
             ysend[rnd, y2] = quarter[:16]
             ysend[rnd, 4 + y2] = quarter[16:]
             for c2 in (c, o) if k else (o,):
@@ -195,14 +201,14 @@
     loads[0].wait()
     st[...] = s[...].T
     pt[0] = st[pl.ds(pl.multiple_of(x * 32, 32), 32), :].reshape(4, 8, HID)
-    loads[1].wait()
 
     def begin(n):
-        if n == 1:
+        loads[1 + n].wait()
+        if n == len(PARTS) - 1:
             pl.semaphore_wait(barrier, 26)
 
     tokens_part(0, begin)
-    loads[2].wait()
+    loads[-1].wait()
 
     def to_row(z2, n):
         span = pl.ds(*PARTS[n])
@@ -237,11 +243,11 @@
 
         rows = [jnp.concatenate([yt[rnd, i * 4 + m] for m in range(4)], axis=1) for i in range(4)]
         lhs = stacked(jnp.concatenate(rows, axis=0))
-        for n in range(2):
-            span = pl.ds(n * 256, 256)
-            part = folded(jnp.dot(lhs, a[:, n * 256 : n * 256 + 256], preferred_element_type=F32))
+        for n, (lo, size) in enumerate(HALVES):
+            span = pl.ds(lo, size)
+            part = folded(jnp.dot(lhs, a[:, lo : lo + size], preferred_element_type=F32))
             for i in range(8):
-                ms[rnd, i, :, n * 256 : n * 256 + 256] = part[i * 8 : i * 8 + 8]
+                ms[rnd, i, :, lo : lo + size] = part[i * 8 : i * 8 + 8]
             for z2, h2 in zh_peers:
                 send(
                     ms.at[rnd, h2 * 4 + z2, :, span], mrs.at[rnd, mine_hz, :, span], rnd, MR[n], dev(z2, x, h2, y, c)
@@ -252,11 +258,11 @@
         def _():
             factor_blocks(9, 14)
 
-        for n in range(2):
-            span = pl.ds(n * 256, 256)
+        for n, (lo, size) in enumerate(HALVES):
+            span = pl.ds(lo, size)
             landed(mrs.at[rnd, pl.ds(0, 7), :, span], rnd, MR[n])
-            got = [mrs[rnd, i, :, n * 256 : n * 256 + 256] for i in range(8)]
-            mraw[rnd, c, mine_hz, :, n * 256 : n * 256 + 256] = ((got[0] + got[1]) + (got[2] + got[3])) + (
+            got = [mrs[rnd, i, :, lo : lo + size] for i in range(8)]
+            mraw[rnd, c, mine_hz, :, lo : lo + size] = ((got[0] + got[1]) + (got[2] + got[3])) + (
                 (got[4] + got[5]) + (got[6] + got[7])
             )
             for z2, h2 in zh_peers:
@@ -267,8 +273,8 @@
         def _():
             factor_blocks(14, 16)
 
-        for n in range(2):
-            landed(mraw.at[rnd, c, pl.ds(0, 7), :, pl.ds(n * 256, 256)], rnd, MG[n])
+        for n, (lo, size) in enumerate(HALVES):
+            landed(mraw.at[rnd, c, pl.ds(0, 7), :, pl.ds(lo, size)], rnd, MG[n])
         send(mraw.at[rnd, c], mraw.at[rnd, c], rnd, MC, partner)
 
         def all_columns():
@@ -387,12 +393,13 @@
     landed(gfull.at[last, o], last, GC)
     factor_start(last)
     factor_blocks(0, 2)
-    for n in range(2):
+    for n in range(len(PARTS)):
         for k in (1, 3, 2):
             z2 = (z + k) % 4
             gathered_p(last, n, z2)
             to_row(z2, n)
-        factor_blocks(2 + n * 2, 4 + n * 2)
+        if n == 0:
+            factor_blocks(2, 4)
     landed(mg.at[pl.ds(0, 3), 0], 0, PHASES)
     for y2 in y_peers:
         piece = mg.at[y2, c]
@@ -400,7 +407,7 @@
     for cc in range(2):
         mg[y, cc] = mt[last, :, cc * 256 : cc * 256 + 256]
     cf[x] = pt[ROUNDS]
-    factor_blocks(6, 16)
+    factor_blocks(4, 16)
     final = work[:, RANK:]
     scaled = final * math.sqrt(D)
     landed(mg.at[pl.ds(0, 3), 0], 1, PHASES)
@@ -416,8 +423,8 @@
     def drain(rnd, carry):
         left(yrs.at[rnd, pl.ds(0, 7)], rnd, YR)
         left(yt.at[rnd, pl.ds(0, 15)], rnd, YG)
-        for n in range(2):
-            span = pl.ds(n * 256, 256)
+        for n, (lo, size) in enumerate(HALVES):
+            span = pl.ds(lo, size)
             left(mrs.at[rnd, pl.ds(0, 7), :, span], rnd, MR[n])
             left(mraw.at[rnd, 0, pl.ds(0, 7), :, span], rnd, MG[n])
         left(mraw.at[rnd, 0], rnd, MC)
@@ -482,14 +489,14 @@
             vm((RANK, 2 * RANK), F32),
             vm((4, 4, 8, HID), F32),
             vm((4, 2, RANK, 256), F32),
-            pltpu.SemaphoreType.DMA((3,)),
+            pltpu.SemaphoreType.DMA((2 + len(PARTS),)),
             pltpu.SemaphoreType.DMA((n, PHASES + 1)),
             pltpu.SemaphoreType.DMA((n, PHASES + 1)),
         ],
         compiler_params=pltpu.CompilerParams(
             collective_id=0, has_side_effects=True, vmem_limit_bytes=50 * 2**20
         ),
-    )(activations, grad_out, sketch)
+    )(activations, grad_out, pltpu.with_memory_space_constraint(sketch, pltpu.HBM))
 
 
 def solution(mesh):

time: 157 us -> 155 us (0.987)
  no operation moved by 1% of the time
where the time goes in v7:
time: 155 us
  Pallas kernels  153 us (99%)
  local copies, waits for them, and re-layouts  1.87 us (1%)
    pallas_call x1, Pallas kernels, body(): pl.pallas_call(kernel, name='range_finder', out_shape=(jax.ShapeDtypeStru...  153 us

profile of v7, /device:TPU:1, one launch (start us, length us, event | category | flops | bytes accessed | tf_op | source)
XLA Modules:
  0.0 155.4 jit_solution(17055682308117313954)
XLA Ops:
  0.6 152.9 %range_finder.1 = (f32[2048,128]{1,0:T(8,128)S(1)}, f32[128,1664]{1,0:T(8,128)S(1)}) custom-call(bf16[1024,2048]{1,0:T(8,128)(2,1)} %a_hbm.1, bf16[1024,1664]{1,0:T(8,128)(2,1)} %b_hbm.1, f32[1664,128]{1,0:T(8,128)} %s_hbm.1), custom_call_target="tpu_custom_call" | custom-call | tf_op jit(solution)/shard_map/range_finder/pallas_call | solution.py:454
  153.5 1.0 copy.7
  154.5 0.9 copy.8

commit v8 on v7

--- a/solution.py
+++ b/solution.py
@@ -20,12 +20,14 @@
 FEAT = 512
 NT = (((1,), (1,)), ((), ()))
 TN = (((0,), (0,)), ((), ()))
-PARTS = ((0, 640), (640, 512), (1152, 512))
+PARTS = ((0, 256), (256, 384), (640, 384), (1024, 384), (1408, 256))
 HALVES = ((0, 256), (256, 256))
 YR, YG, MC, XR, XG, GY, GX, GZ, GC = range(9)
-MR, MG, PR = range(9, 12), range(12, 15), range(15, 18)
-PG = range(18, 30, 4)
-PHASES = 30
+MR = range(9, 9 + len(HALVES))
+MG = range(MR.stop, MR.stop + len(HALVES))
+PR = range(MG.stop, MG.stop + len(PARTS))
+PG = range(PR.stop, PR.stop + 4 * len(PARTS), 4)
+PHASES = PG.stop
 XY = (
     (2, 2), (2, 1), (2, 3), (1, 2), (3, 2), (1, 1), (1, 3), (3, 1), (3, 3),
     (2, 0), (0, 2), (1, 0), (3, 0), (0, 1), (0, 3),
@@ -219,6 +221,10 @@
         lo, size = PARTS[n]
         landed(pt.at[rnd + 1, z2, :, pl.ds(lo, size)], rnd, PG[n] + z2)
 
+    def share_gram(rnd):
+        landed(gfull.at[rnd, c, pl.ds(0, 3)], rnd, GZ)
+        send(gfull.at[rnd, c], gfull.at[rnd, c], rnd, GC, partner)
+
     def one_round(rnd, carry):
         yrs[rnd, mine_cy] = ysend[rnd, mine_cy]
 
@@ -361,6 +367,12 @@
                     dev(z, x, h, y2, c),
                 )
 
+        @pl.when(rnd == ROUNDS - 1)
+        def _():
+            share_gram(rnd)
+            landed(gfull.at[rnd, o], rnd, GC)
+            factor_start(rnd)
+
         for n, (lo, size) in enumerate(PARTS):
             span = pl.ds(lo, size)
             landed(prs.at[rnd, pl.ds(0, 3), :, span], rnd, PR[n])
@@ -373,12 +385,13 @@
             @pl.when(rnd == ROUNDS - 1)
             def _():
                 to_row(z, n)
-
-        landed(gfull.at[rnd, c, pl.ds(0, 3)], rnd, GZ)
-        send(gfull.at[rnd, c], gfull.at[rnd, c], rnd, GC, partner)
+                factor_blocks(n * 6 // len(PARTS), (n + 1) * 6 // len(PARTS))
+
 
         @pl.when(rnd < ROUNDS - 1)
         def _():
+            share_gram(rnd)
+
             def ready(n):
                 for z2 in z_peers:
                     gathered_p(rnd, n, z2)
@@ -390,16 +403,15 @@
     lax.fori_loop(0, ROUNDS, one_round, 0)
 
     last = ROUNDS - 1
-    landed(gfull.at[last, o], last, GC)
-    factor_start(last)
-    factor_blocks(0, 2)
+    done = 6
     for n in range(len(PARTS)):
         for k in (1, 3, 2):
             z2 = (z + k) % 4
             gathered_p(last, n, z2)
             to_row(z2, n)
-        if n == 0:
-            factor_blocks(2, 4)
+        if n < len(PARTS) - 1:
+            factor_blocks(done, done + 1)
+            done += 1
     landed(mg.at[pl.ds(0, 3), 0], 0, PHASES)
     for y2 in y_peers:
         piece = mg.at[y2, c]
@@ -407,7 +419,7 @@
     for cc in range(2):
         mg[y, cc] = mt[last, :, cc * 256 : cc * 256 + 256]
     cf[x] = pt[ROUNDS]
-    factor_blocks(4, 16)
+    factor_blocks(done, 16)
     final = work[:, RANK:]
     scaled = final * math.sqrt(D)
     landed(mg.at[pl.ds(0, 3), 0], 1, PHASES)

time: 155 us -> 153 us (0.987)
  Pallas kernels: 153 us -> 150 us
    pallas_call x1, Pallas kernels: 153 us -> 150 us  [body(): pl.pallas_call(kernel, name='range_finder', out_shape=(jax.ShapeDtypeStru...]
where the time goes in v8:
time: 153 us
  Pallas kernels  150 us (98%)
  local copies, waits for them, and re-layouts  1.87 us (1%)
    pallas_call x1, Pallas kernels, body(): pl.pallas_call(kernel, name='range_finder', out_shape=(jax.ShapeDtypeStru...  150 us

profile of v8, /device:TPU:1, one launch (start us, length us, event | category | flops | bytes accessed | tf_op | source)
XLA Modules:
  0.0 152.9 jit_solution(6117400733355370429)
XLA Ops:
  0.6 150.4 %range_finder.1 = (f32[2048,128]{1,0:T(8,128)S(1)}, f32[128,1664]{1,0:T(8,128)S(1)}) custom-call(bf16[1024,2048]{1,0:T(8,128)(2,1)} %a_hbm.1, bf16[1024,1664]{1,0:T(8,128)(2,1)} %b_hbm.1, f32[1664,128]{1,0:T(8,128)} %s_hbm.1), custom_call_target="tpu_custom_call" | custom-call | tf_op jit(solution)/shard_map/range_finder/pallas_call | solution.py:466
  151.1 1.0 copy.7
  152.0 0.9 copy.8

commit v9 on v8

--- a/solution.py
+++ b/solution.py
@@ -215,7 +215,7 @@
     def to_row(z2, n):
         span = pl.ds(*PARTS[n])
         for x2 in x_peers:
-            send(pt.at[ROUNDS, z2, :, span], cf.at[x, z2, :, span], 2, PHASES, dev(z, x2, h, y, c))
+            send(pt.at[ROUNDS, z2, :, span], cf.at[x, z2, :, span], 2, PHASES + 1 + n, dev(z, x2, h, y, c))
 
     def gathered_p(rnd, n, z2):
         lo, size = PARTS[n]
@@ -429,8 +429,11 @@
             basis_ref[r0 : r0 + 256, :] = lax.dot_general(
                 mg[i, cc].T, scaled, NT, precision=HIGHEST, preferred_element_type=F32
             )
-    landed(cf.at[pl.ds(0, 3)], 2, PHASES)
-    coef_ref[...] = jnp.dot(final, cf[...].reshape(RANK, HID), precision=HIGHEST, preferred_element_type=F32)
+    for n, (lo, size) in enumerate(PARTS):
+        landed(cf.at[pl.ds(0, 3), :, :, pl.ds(lo, size)], 2, PHASES + 1 + n)
+        coef_ref[:, lo : lo + size] = jnp.dot(
+            final, cf[:, :, :, lo : lo + size].reshape(RANK, size), precision=HIGHEST, preferred_element_type=F32
+        )
 
     def drain(rnd, carry):
         left(yrs.at[rnd, pl.ds(0, 7)], rnd, YR)
@@ -455,7 +458,19 @@
     lax.fori_loop(0, ROUNDS, drain, 0)
     left(mg.at[pl.ds(0, 3), 0], 0, PHASES)
     left(mg.at[pl.ds(0, 3), 0], 1, PHASES)
-    left(cf.at[pl.ds(0, 3)], 2, PHASES)
+    for n, (lo, size) in enumerate(PARTS):
+        left(cf.at[pl.ds(0, 3), :, :, pl.ds(lo, size)], 2, PHASES + 1 + n)
+
+
+def hand_over(basis_in, coef_in, basis_out, coef_out, sem):
+    copies = [
+        pltpu.make_async_copy(basis_in, basis_out, sem.at[0]),
+        pltpu.make_async_copy(coef_in, coef_out, sem.at[1]),
+    ]
+    for copy in copies:
+        copy.start()
+    for copy in copies:
+        copy.wait()
 
 
 def body(activations, grad_out, sketch):
@@ -463,13 +478,14 @@
     inside = pl.BlockSpec(memory_space=pltpu.VMEM)
     vm = pltpu.VMEM
     n = ROUNDS
-    return pl.pallas_call(
+    shapes = (
+        jax.ShapeDtypeStruct((2048, RANK), F32),
+        jax.ShapeDtypeStruct((RANK, HID), F32),
+    )
+    found = pl.pallas_call(
         kernel,
         name="range_finder",
-        out_shape=(
-            jax.ShapeDtypeStruct((2048, RANK), F32),
-            jax.ShapeDtypeStruct((RANK, HID), F32),
-        ),
+        out_shape=shapes,
         in_specs=[anywhere] * 3,
         out_specs=(inside, inside),
         scratch_shapes=[
@@ -502,13 +518,22 @@
             vm((4, 4, 8, HID), F32),
             vm((4, 2, RANK, 256), F32),
             pltpu.SemaphoreType.DMA((2 + len(PARTS),)),
-            pltpu.SemaphoreType.DMA((n, PHASES + 1)),
-            pltpu.SemaphoreType.DMA((n, PHASES + 1)),
+            pltpu.SemaphoreType.DMA((n, PHASES + 1 + len(PARTS))),
+            pltpu.SemaphoreType.DMA((n, PHASES + 1 + len(PARTS))),
         ],
         compiler_params=pltpu.CompilerParams(
             collective_id=0, has_side_effects=True, vmem_limit_bytes=50 * 2**20
         ),
     )(activations, grad_out, pltpu.with_memory_space_constraint(sketch, pltpu.HBM))
+    return pl.pallas_call(
+        hand_over,
+        name="hand_over",
+        out_shape=shapes,
+        in_specs=[anywhere] * 2,
+        out_specs=(anywhere, anywhere),
+        scratch_shapes=[pltpu.SemaphoreType.DMA((2,))],
+        cost_estimate=pl.CostEstimate(flops=0, bytes_accessed=4 * 2**20, transcendentals=0),
+    )(*found)
 
 
 def solution(mesh):

time: 153 us -> 211 us (1.38)
  Pallas kernels: 150 us -> 209 us
    pallas_call x1 -> x2, Pallas kernels: 150 us -> 209 us  [the longest x1 150 us: body(): pl.pallas_call(kernel, name='range_finder', out_shape=shapes, in_specs=[a...]
where the time goes in v9:
time: 211 us
  Pallas kernels  209 us (99%)
    pallas_call x1, Pallas kernels, body(): pl.pallas_call(kernel, name='range_finder', out_shape=shapes, in_specs=[a...  150 us
    pallas_call x1, Pallas kernels, body(): pl.pallas_call(hand_over, name='hand_over', out_shape=shapes, in_specs=[a...  58.7 us

profile of v9, /device:TPU:1, one launch (start us, length us, event | category | flops | bytes accessed | tf_op | source)
XLA Modules:
  0.0 211.4 jit_solution(12823619726831558323)
XLA Ops:
  0.6 150.2 %range_finder.1 = (f32[2048,128]{1,0:T(8,128)S(1)}, f32[128,1664]{1,0:T(8,128)S(1)}) custom-call(bf16[1024,2048]{1,0:T(8,128)(2,1)} %a_hbm.1, bf16[1024,1664]{1,0:T(8,128)(2,1)} %b_hbm.1, f32[1664,128]{1,0:T(8,128)} %s_hbm.1), custom_call_target="tpu_custom_call" | custom-call | tf_op jit(solution)/shard_map/range_finder/pallas_call | solution.py:485
  150.8 0.0 copy-start
  150.8 1.0 copy-done
  151.8 0.0 copy-start.1
  151.8 0.9 copy-done.1
  152.7 58.7 %hand_over.1 = (f32[2048,128]{1,0:T(8,128)}, f32[128,1664]{1,0:T(8,128)}) custom-call(f32[2048,128]{1,0:T(8,128)} %copy-done, f32[128,1664]{1,0:T(8,128)} %copy-done.1), custom_call_target="tpu_custom_call" | custom-call | bytes 4194304 | tf_op jit(solution)/shard_map/hand_over/pallas_call | solution.py:528
Async XLA Ops:
  150.8 1.0 copy-start
  151.8 0.9 copy-start.1

commit v10 on v9

--- a/solution.py
+++ b/solution.py
@@ -462,15 +462,9 @@
         left(cf.at[pl.ds(0, 3), :, :, pl.ds(lo, size)], 2, PHASES + 1 + n)
 
 
-def hand_over(basis_in, coef_in, basis_out, coef_out, sem):
-    copies = [
-        pltpu.make_async_copy(basis_in, basis_out, sem.at[0]),
-        pltpu.make_async_copy(coef_in, coef_out, sem.at[1]),
-    ]
-    for copy in copies:
-        copy.start()
-    for copy in copies:
-        copy.wait()
+def hand_over(basis_in, coef_in, basis_out, coef_out):
+    basis_out[...] = basis_in[...]
+    coef_out[...] = coef_in[...]
 
 
 def body(activations, grad_out, sketch):
@@ -529,9 +523,9 @@
         hand_over,
         name="hand_over",
         out_shape=shapes,
-        in_specs=[anywhere] * 2,
-        out_specs=(anywhere, anywhere),
-        scratch_shapes=[pltpu.SemaphoreType.DMA((2,))],
+        in_specs=[inside] * 2,
+        out_specs=(inside, inside),
+        compiler_params=pltpu.CompilerParams(vmem_limit_bytes=8 * 2**20),
         cost_estimate=pl.CostEstimate(flops=0, bytes_accessed=4 * 2**20, transcendentals=0),
     )(*found)
 

time: 211 us -> 152 us (0.72)
  Pallas kernels: 209 us -> 152 us
    pallas_call x1, Pallas kernels: 58.7 us -> 1.37 us  [body(): pl.pallas_call(hand_over, name='hand_over', out_shape=shapes, in_specs=[i...]
where the time goes in v10:
time: 152 us
  Pallas kernels  152 us (100%)
    pallas_call x1, Pallas kernels, body(): pl.pallas_call(kernel, name='range_finder', out_shape=shapes, in_specs=[a...  150 us

profile of v10, /device:TPU:1, one launch (start us, length us, event | category | flops | bytes accessed | tf_op | source)
XLA Modules:
  0.0 152.2 jit_solution(13906785768093806813)
XLA Ops:
  0.6 150.2 %range_finder.1 = (f32[2048,128]{1,0:T(8,128)S(1)}, f32[128,1664]{1,0:T(8,128)S(1)}) custom-call(bf16[1024,2048]{1,0:T(8,128)(2,1)} %a_hbm.1, bf16[1024,1664]{1,0:T(8,128)(2,1)} %b_hbm.1, f32[1664,128]{1,0:T(8,128)} %s_hbm.1), custom_call_target="tpu_custom_call" | custom-call | tf_op jit(solution)/shard_map/range_finder/pallas_call | solution.py:479
  150.8 1.4 hand_over.1

commit v11 on v10

--- a/solution.py
+++ b/solution.py
@@ -298,9 +298,10 @@
         @pl.when(rnd > 0)
         def _():
             all_columns()
-            mt[rnd] = jnp.dot(work[:, RANK:], mfull[...], precision=HIGHEST, preferred_element_type=F32)
-            for i in range(4):
-                xl[i * 16 : i * 16 + 16, :] = mt[rnd, pl.ds(pl.multiple_of(i * 32 + c * 16, 16), 16), :]
+            rows = [work[pl.ds(pl.multiple_of(i * 32 + c * 16, 16), 16), RANK:] for i in range(4)]
+            xl[...] = jnp.dot(
+                jnp.concatenate(rows, axis=0), mfull[...], precision=HIGHEST, preferred_element_type=F32
+            )
 
         lhs = stacked(xl[...])
         for k in (2, 1, 3, 0):
@@ -317,6 +318,10 @@
         def _():
             all_columns()
             mt[rnd] = mfull[...]
+
+        @pl.when(rnd > 0)
+        def _():
+            mt[rnd] = jnp.dot(work[:, RANK:], mfull[...], precision=HIGHEST, preferred_element_type=F32)
 
         gown[rnd] = lax.dot_general(
             mt[rnd, pl.ds(pl.multiple_of((c * 4 + z) * 16, 16), 16), :],

time: 152 us -> 153 us (level)
  no operation moved by 1% of the time
where the time goes in v11:
time: 153 us
  Pallas kernels  152 us (99%)
    pallas_call x1, Pallas kernels, body(): pl.pallas_call(kernel, name='range_finder', out_shape=shapes, in_specs=[a...  151 us

profile of v11, /device:TPU:1, one launch (start us, length us, event | category | flops | bytes accessed | tf_op | source)
XLA Modules:
  0.0 152.7 jit_solution(8825469054635461603)
XLA Ops:
  0.6 150.6 %range_finder.1 = (f32[2048,128]{1,0:T(8,128)S(1)}, f32[128,1664]{1,0:T(8,128)S(1)}) custom-call(bf16[1024,2048]{1,0:T(8,128)(2,1)} %a_hbm.1, bf16[1024,1664]{1,0:T(8,128)(2,1)} %b_hbm.1, f32[1664,128]{1,0:T(8,128)} %s_hbm.1), custom_call_target="tpu_custom_call" | custom-call | tf_op jit(solution)/shard_map/range_finder/pallas_call | solution.py:484
  151.3 1.4 hand_over.1
